TPU v7x, 256 devices: a whole 4x4x8 slice. The times are simulated.
256 devices in a mesh: dp: 32 (over x_lo, z, core), mp: 8 (over y, x_hi).
Axes of the slice: x: 4 (x_hi: 2, x_lo: 2; x = x_hi * 2 + x_lo), y: 4, z: 8, core: 2. Of those that a mesh axis runs over, the one named last changes fastest.
Arguments:
- student_feats: bfloat16 [96, 112, 1408], P('dp'), may hold values from -7 to 7
- keep_index: int32 [96, 112], P('dp'), may hold values from 0 to 559, as said below
- hidden_six: bfloat16 [96, 560, 12800], P('dp', None, 'mp'), may hold values from -6 to 6
- resid_six: bfloat16 [96, 560, 3200], P('dp', None, 'mp'), may hold values from -32 to 32
- down_six: bfloat16 [12800, 3200], P('mp', 'dp'), may hold values from -0.0546875 to 0.0546875
- hidden_giant: bfloat16 [96, 560, 6144], P('dp', None, 'mp'), may hold values from -6 to 6
- resid_giant: bfloat16 [96, 560, 1408], P('dp', None, 'mp'), may hold values from -32 to 32
- down_giant: bfloat16 [6144, 1408], P('mp', 'dp'), may hold values from -0.078125 to 0.078125
- proj_six: bfloat16 [1408, 3200], P(None, 'mp'), may hold values from -5 to 5
- proj_giant: bfloat16 [1408, 1408], P(None, 'mp'), may hold values from -5 to 5
Outputs:
- grad_student: float32 [96, 112, 1408], P('dp', None, 'mp')
- grad_proj_six: float32 [1408, 3200], P(None, 'mp')
- grad_proj_giant: float32 [1408, 1408], P(None, 'mp')
- loss: float32 [], replicated
Inputs may be any that keep to these rules, and one draw needn't show every extreme that they name: `keep_index`: each row holds 112 distinct positions of the clip's tokens in rising order.
All inputs are finite; a program needn't handle non-finite values.
Results may differ from a plain program's by a relative error of at most 0.015.
Values may be sent and summed in bfloat16 or wider, within the bound.
A program may use at most 128 MiB of HBM per device.

v0:
```python
import jax
import jax.numpy as jnp
from jax import lax
from jax.sharding import PartitionSpec as P

loss_scale = 256.0
head_scale = 64.0
norm_eps = 1e-06


def select_kept(values, keep_index):
    chosen = jnp.take_along_axis(values, keep_index[:, :, None], axis=1)
    return chosen.reshape(-1, values.shape[2])


def head_gradient(outputs, target, inner, out_square, tar_square):
    norm_out = jnp.sqrt(out_square + norm_eps)
    norm_tar = jnp.sqrt(tar_square + norm_eps)
    cosine = inner / (norm_out * norm_tar)
    grad_out = -loss_scale * (
        target / (norm_out * norm_tar)[:, None]
        - (cosine / (norm_out * norm_out))[:, None] * outputs
    )
    return (cosine, grad_out.astype(jnp.bfloat16))


def local(
    student_feats,
    keep_index,
    hidden_six,
    resid_six,
    down_six,
    hidden_giant,
    resid_giant,
    down_giant,
    proj_six,
    proj_giant,
):
    clip_count, kept_count = keep_index.shape
    rows_six = select_kept(hidden_six, keep_index)
    rows_giant = select_kept(hidden_giant, keep_index)
    shard_count = lax.axis_size("dp")
    part_six = jnp.dot(
        rows_six,
        lax.all_gather(down_six, "dp", axis=1, tiled=True),
        preferred_element_type=jnp.float32,
    )
    part_giant = jnp.dot(
        rows_giant,
        lax.all_gather(down_giant, "dp", axis=1, tiled=True),
        preferred_element_type=jnp.float32,
    )
    summed_six, summed_giant = (
        lax.psum_scatter(
            part_six.astype(jnp.bfloat16), "mp", scatter_dimension=1, tiled=True
        ).astype(jnp.float32),
        lax.psum_scatter(
            part_giant.astype(jnp.bfloat16), "mp", scatter_dimension=1, tiled=True
        ).astype(jnp.float32),
    )
    target_six = summed_six + select_kept(resid_six, keep_index).astype(jnp.float32)
    target_giant = summed_giant + select_kept(resid_giant, keep_index).astype(jnp.float32)
    student_rows = student_feats.reshape(-1, student_feats.shape[2])
    out_six = jnp.dot(student_rows, proj_six, preferred_element_type=jnp.float32)
    out_giant = jnp.dot(student_rows, proj_giant, preferred_element_type=jnp.float32)
    local_stats = jnp.stack(
        [
            jnp.sum(out_six * target_six, axis=1),
            jnp.sum(out_six * out_six, axis=1),
            jnp.sum(target_six * target_six, axis=1),
            jnp.sum(out_giant * target_giant, axis=1),
            jnp.sum(out_giant * out_giant, axis=1),
            jnp.sum(target_giant * target_giant, axis=1),
        ]
    )
    stats = lax.psum(local_stats, "mp")
    cosine_six, grad_six = head_gradient(out_six, target_six, stats[0], stats[1], stats[2])
    cosine_giant, grad_giant = head_gradient(out_giant, target_giant, stats[3], stats[4], stats[5])
    loss_local = jnp.sum(2.0 - cosine_six - cosine_giant)
    contract_rows = (((0,), (0,)), ((), ()))
    head_six = lax.dot_general(
        student_rows, grad_six, contract_rows, preferred_element_type=jnp.float32
    )
    head_giant = lax.dot_general(
        student_rows, grad_giant, contract_rows, preferred_element_type=jnp.float32
    )
    summed_head_six, summed_head_giant, loss_total = lax.psum(
        (head_six, head_giant, loss_local), "dp"
    )
    token_total = student_rows.shape[0] * shard_count
    grad_proj_six = summed_head_six * (head_scale / token_total)
    grad_proj_giant = summed_head_giant * (head_scale / token_total)
    loss = loss_total / token_total
    contract_cols = (((1,), (1,)), ((), ()))
    back_rows = lax.dot_general(
        grad_six, proj_six, contract_cols, preferred_element_type=jnp.float32
    )
    back_rows = back_rows + lax.dot_general(
        grad_giant, proj_giant, contract_cols, preferred_element_type=jnp.float32
    )
    grad_rows = lax.psum_scatter(back_rows, "mp", scatter_dimension=1, tiled=True)
    grad_student = grad_rows.reshape(clip_count, kept_count, -1)
    return (grad_student, grad_proj_six, grad_proj_giant, loss)


def solution(mesh):
    return jax.shard_map(
        local,
        mesh=mesh,
        in_specs=(
            P("dp", None, None),
            P("dp", None),
            P("dp", None, "mp"),
            P("dp", None, "mp"),
            P("mp", "dp"),
            P("dp", None, "mp"),
            P("dp", None, "mp"),
            P("mp", "dp"),
            P(None, "mp"),
            P(None, "mp"),
        ),
        out_specs=(P("dp", None, "mp"), P(None, "mp"), P(None, "mp"), P()),
        check_vma=False,
    )
```

profile of v0, /device:TPU:1, one launch (start us, length us, event | category | flops | bytes accessed | tf_op | source)
XLA Modules:
  0.0 688.8 jit_solution(13485613872550639750)
XLA Ops:
  7.2 0.7 all-gather.7.cloned.1.call-update
  8.0 0.7 all-gather.5.cloned.1.call-update
  8.7 0.7 compare_and_fusion
  9.4 0.1 broadcast_in_dim.42
  9.5 0.7 bitcast_or_fusion
  10.2 0.1 reshape.105
  10.3 6.2 gather_fusion.2
  16.4 62.9 %all-gather.7.cloned.1.call-done = bf16[32,44,768]{2,1,0:T(8,128)(2,1)} async-done(((bf16[1,44,768]{2,1,0:T(8,128)(2,1)}), bf16[32,44,768]{2,1,0:T(8,128)(2,1)}) %all-gather.7.cloned.1.call-update) | async-done | bytes 2162704 | tf_op jit(solution)/shard_map/all_gather | solution.py:50
  79.3 4.0 reshape.141
  83.3 4.0 convolution_convert_fusion.1
  87.4 14.4 %gather_fusion = bf16[336,1600]{1,0:T(8,128)(2,1)} fusion(bf16[3,560,1600]{2,1,0:T(8,128)(2,1)} %param.12, s32[336]{0:T(512)S(1)} %reshape.105), kind=kCustom, calls=%fused_computation | custom fusion | bytes 2153088 | tf_op jit(solution)/shard_map/jit(take_along_axis)/gather | solution.py:12
  101.7 55.7 %all-gather.5.cloned.1.call-done = bf16[32,100,1600]{2,1,0:T(8,128)(2,1)} async-done(((bf16[1,100,1600]{2,1,0:T(8,128)(2,1)}), bf16[32,100,1600]{2,1,0:T(8,128)(2,1)}) %all-gather.5.cloned.1.call-update) | async-done | bytes 10240016 | tf_op jit(solution)/shard_map/all_gather | solution.py:45
  157.5 14.6 %reshape.139 = bf16[3200,1600]{1,0:T(8,128)(2,1)} reshape(bf16[32,100,1600]{2,1,0:T(8,128)(2,1)} %all-gather.5.cloned.1.call-done) | data formatting | bytes 20480000
  172.1 10.2 %convolution_convert_fusion = bf16[336,3200]{0,1:T(8,128)(2,1)} fusion(bf16[3200,1600]{1,0:T(8,128)(2,1)} %reshape.139, bf16[336,1600]{1,0:T(8,128)(2,1)} %gather_fusion, pred[336]{0:T(512)(128)(4,1)S(1)} %broadcast_in_dim.42), kind=kOutput, calls=%fused_computation.4 | convolution fusion | flops 3442252800 | bytes 13465936 | tf_op jit(solution)/shard_map/dot_general | solution.py:43
  182.3 0.2 all-reduce.3.cloned.1.call-start
  182.6 1.4 copy.26
  184.0 6.1 gather_fusion.3
  190.1 1.7 copy.27
  191.8 3.7 copy.24
  195.5 12.4 %gather_fusion.1 = bf16[336,400]{1,0:T(8,128)(2,1)} fusion(bf16[3,560,400]{2,1,0:T(8,128)(2,1)} %copy.24, s32[336]{0:T(512)S(1)} %reshape.105), kind=kCustom, calls=%fused_computation.1 | custom fusion | bytes 540288 | tf_op jit(solution)/shard_map/jit(take_along_axis)/gather | solution.py:12
  207.9 1.9 copy.25
  209.8 24.3 %reduce-scatter.6.cloned.1.call-done = bf16[336,176]{0,1:T(8,128)(2,1)} async-done(((bf16[336,1408]{0,1:T(8,128)(2,1)}), bf16[336,176]{0,1:T(8,128)(2,1)}) %reduce-scatter.6.cloned.1.call-update) | async-done | bytes 118288 | tf_op jit(solution)/shard_map/reduce_scatter | solution.py:57
  234.0 2.4 multiply_reduce_fusion.3
  236.4 81.7 %reduce-scatter.4.cloned.1.call-done = bf16[336,400]{0,1:T(8,128)(2,1)} async-done(((bf16[336,3200]{0,1:T(8,128)(2,1)}), bf16[336,400]{0,1:T(8,128)(2,1)}) %reduce-scatter.4.cloned.1.call-update) | async-done | bytes 268816 | tf_op jit(solution)/shard_map/reduce_scatter | solution.py:54
  318.1 3.0 multiply_reduce_fusion
  321.2 0.6 stack.21
  321.7 0.6 stack.22
  322.3 0.7 stack.27
  323.1 32.2 %psum.28 = f32[6,336]{1,0:T(8,128)S(1)} all-reduce(f32[6,336]{1,0:T(8,128)S(1)} %stack.27), channel_id=1, replica_groups=mesh['dp'=32,'mp'=8] {'mp'}, use_global_device_ids=true, to_apply=%region_8.9 | all-reduce | flops 2016 | bytes 16128 | tf_op jit(solution)/shard_map/psum | solution.py:76
  355.3 0.1 multiply_reduce_fusion.7
  355.3 0.6 subtract_reduce_fusion
  355.9 1.1 multiply_convert_fusion.1
  357.1 1.4 convolution_bitcast_fusion.1
  358.5 0.2 multiply_convert_fusion
  358.7 0.7 copy-done.2
  359.4 2.2 convolution_bitcast_fusion
  361.7 0.8 copy-done.6
  362.5 0.2 copy-done.9
  362.7 0.6 fusion.16
  363.3 0.6 copy-done.7
  364.0 2.3 convolution_add_fusion
  366.3 62.2 %psum.31 = f32[]{:T(128)} all-reduce(f32[]{:T(128)} %get-tuple-element.30), channel_id=1, replica_groups=mesh['dp'=32,'mp'=8] {'dp'}, use_global_device_ids=true, to_apply=%region_13.14 | all-reduce | flops 1 | bytes 8 | tf_op jit(solution)/shard_map/psum | solution.py:87
  429.2 168.2 %all-reduce.3.cloned.1.call-done = (f32[1408,400]{0,1:T(8,128)}, f32[1408,176]{0,1:T(8,128)}) async-done(((f32[1408,400]{0,1:T(8,128)}, f32[1408,176]{0,1:T(8,128)}), (f32[1408,400]{0,1:T(8,128)}, f32[1408,176]{0,1:T(8,128)})) %all-reduce.3.cloned.1.call-update) | async-done | bytes 3244048 | tf_op jit(solution)/shard_map/psum | solution.py:87
  597.4 2.2 broadcast_multiply_fusion.1
  599.6 3.2 broadcast_multiply_fusion
  602.8 76.1 %reduce-scatter.8.cloned.1.call-done = f32[336,176]{0,1:T(8,128)} async-done(((f32[336,1408]{0,1:T(8,128)}), f32[336,176]{0,1:T(8,128)}) %reduce-scatter.8.cloned.1.call-update) | async-done | bytes 236560 | tf_op jit(solution)/shard_map/reduce_scatter | solution.py:101
  678.9 1.2 reshape.104
  680.1 0.7 copy.28
  (35 shorter events, 0.3 us)
Async XLA Ops:
  7.2 3.1 copy-start
  7.2 72.1 %all-gather.7.cloned.1.call-start = ((), (), s32[]{:S(2)}) async-start(), calls=%async_computation.7 | async-start | bytes 2433024 | tf_op jit(solution)/shard_map/all_gather | solution.py:50
  7.9 149.6 %all-gather.5.cloned.1.call-start = ((), (), s32[]{:S(2)}) async-start(), calls=%async_computation.6 | async-start | bytes 11421696 | tf_op jit(solution)/shard_map/all_gather | solution.py:45
  8.7 225.4 %reduce-scatter.6.cloned.1.call-start = ((), (), s32[]{:S(2)}) async-start(), calls=%async_computation.4 | async-start | bytes 1216512 | tf_op jit(solution)/shard_map/reduce_scatter | solution.py:57
  9.5 308.6 %copy-start.11 = (pred[336]{0:T(512)(128)(4,1)}, pred[336]{0:T(512)(128)(4,1)S(1)}, u32[]{:S(2)}) copy-start(pred[336]{0:T(512)(128)(4,1)S(1)} %broadcast_in_dim.42) | copy-start | bytes 1012
  87.3 230.8 %reduce-scatter.4.cloned.1.call-start = ((), (), s32[]{:S(2)}) async-start(), calls=%async_computation.3 | async-start | bytes 2764800 | tf_op jit(solution)/shard_map/reduce_scatter | solution.py:54
  182.3 415.0 %all-reduce.3.cloned.1.call-start = ((), (), s32[]{:S(2)}) async-start(), calls=%async_computation.8 | async-start | bytes 6488064 | tf_op jit(solution)/shard_map/psum | solution.py:87
  195.5 38.6 %copy-start.1 = (bf16[3,112,1408]{2,1,0:T(8,128)(2,1)S(1)}, bf16[3,112,1408]{2,1,0:T(8,128)(2,1)}, u32[]{:S(2)}) copy-start(bf16[3,112,1408]{2,1,0:T(8,128)(2,1)} %param.10) | copy-start | bytes 2838532
  323.1 35.4 %copy-start.12 = (pred[336]{0:T(512)(128)(4,1)S(1)}, pred[336]{0:T(512)(128)(4,1)}, u32[]{:S(2)}) copy-start(pred[336]{0:T(512)(128)(4,1)} %copy-done.11) | copy-start | bytes 1012
  355.3 3.2 copy-start.4
  355.3 3.2 copy-start.8
  355.3 3.2 copy-start.10
  357.1 1.4 copy-start.5
  358.7 0.7 copy-start.2
  361.6 0.9 copy-start.6
  361.6 1.1 copy-start.9
  361.6 1.7 copy-start.3
  361.6 317.3 %reduce-scatter.8.cloned.1.call-start = ((), (), s32[]{:S(2)}) async-start(), calls=%async_computation.5 | async-start | bytes 2433024 | tf_op jit(solution)/shard_map/reduce_scatter | solution.py:101
  362.7 1.3 copy-start.7
Sparse Core Ops, SparseCore 0:
  9.9 69.3 all-gather.6
  81.2 76.2 all-gather.4
  161.4 72.5 reduce-scatter.5
  238.1 79.9 reduce-scatter.3
  361.7 235.5 all-reduce.2
  601.8 77.0 reduce-scatter.7
where the time goes:
time: 690 us; the launch traced here: 689 us
  waiting for transfers between devices  470 us (68%)
  blocking collectives  94.4 us (14%)
  local copies, waits for them, and re-layouts  72.7 us (11%)
  matrix products  26.2 us (4%)
  between operations  16 us (2%)
  other arithmetic  8.82 us (1%)
    psum x1, waiting for transfers between devices, local(): lax.psum((head_six, head_giant, loss_local), 'dp')  168 us
    reduce_scatter x1, waiting for transfers between devices, local(): lax.psum_scatter(part_six.astype(jnp.bfloat16), 'mp', scatter_dimension=1...  81.7 us
    reduce_scatter x1, waiting for transfers between devices, local(): lax.psum_scatter(back_rows, 'mp', scatter_dimension=1, tiled=True)  76.1 us
    all_gather x1, waiting for transfers between devices, local(): lax.all_gather(down_giant, 'dp', axis=1, tiled=True)  62.9 us
    psum x1, blocking collectives, local(): lax.psum((head_six, head_giant, loss_local), 'dp')  62.2 us
    all_gather x1, waiting for transfers between devices, local(): lax.all_gather(down_six, 'dp', axis=1, tiled=True)  55.7 us
    gather x7, local copies, waits for them, and re-layouts, select_kept(): chosen = jnp.take_along_axis(values, keep_index[:, :, None], axis=1)  42.7 us
    psum x1, blocking collectives, local(): stats = lax.psum(local_stats, 'mp')  32.2 us
  transfers between devices with their start and end apart: 6, of which 6 were waited for; matrix products, arithmetic and copies ran while one was open for 13% of the time, Pallas kernels for 0%

commit v1 on v0

v1 whole, which is shorter than its diff:
```python
import functools

import jax
import jax.numpy as jnp
from jax import lax
from jax.experimental import pallas as pl
from jax.experimental.pallas import tpu as pltpu
from jax.sharding import PartitionSpec as P

loss_scale = 256.0
head_scale = 64.0
norm_eps = 1e-06

NZ = 8
NY = 4
F32 = jnp.float32
BF16 = jnp.bfloat16
MESH = pl.DeviceIdType.MESH

SENDS = (
    ((0, 0), (0, 0), (0, 0)),
    ((0, -1), (0, 1), (0, -1)),
    ((0, -2), (0, 2), (0, -2)),
    ((0, -3), (1, 0), (0, 3)),
    ((1, -2), (1, 1), (0, 4)),
)
RECVS = (
    ((0, -1), (0, 1), (1, 0)),
    ((0, -2), (0, 2), (1, -1)),
    ((0, -3), (0, 3), (1, -2)),
    ((0, -4), (1, 1), (1, 3)),
    ((1, -3), (1, 2), (1, 4)),
)
STEPS = len(SENDS)
OWN = 3 * STEPS
Z_ORDER = (4, 3, 5, 2, 6, 1, 7)


def nt(a, b):
    return lax.dot_general(a, b, (((1,), (1,)), ((), ())), preferred_element_type=F32)


def nn(a, b):
    return lax.dot_general(a, b, (((1,), (0,)), ((), ())), preferred_element_type=F32)


def kernel(
    token_total,
    keep_row,
    keep_col,
    stu_hbm,
    h6_hbm,
    r6_hbm,
    w6_hbm,
    hg_hbm,
    rg_hbm,
    wg_hbm,
    p6_hbm,
    pg_hbm,
    gp6_out,
    gpg_out,
    back_out,
    loss_out,
    w6_in,
    wg_in,
    gath6,
    gathg,
    h6,
    hg,
    r6,
    rg,
    rows6,
    rowsg,
    stu,
    pt,
    pmat,
    part,
    yrecv,
    xsend,
    xrecv,
    tgt,
    outs,
    stats,
    grad,
    gs,
    grecv,
    gxs,
    gxr,
    gzs,
    gzr,
    ag,
    fout,
    bsend,
    byr,
    bxs,
    bxr,
    bfin,
    lossz,
    lossx,
    lossc,
    lossv,
    load_sem,
    wsend_sem,
    wrecv_sem,
    psend_sem,
    precv_sem,
    ysend_sem,
    yrecv_sem,
    xh_sem,
    st_sem,
    g_sem,
    agz_sem,
    agx_sem,
    agp_sem,
    b_sem,
    l_sem,
    out_sem,
):
    dp = lax.axis_index("dp")
    mp = lax.axis_index("mp")
    c = dp % 2
    z = (dp // 2) % NZ
    xl = dp // (2 * NZ)
    y = mp // 2
    xh = mp % 2

    pair = {"dp": dp + 1 - 2 * c}
    xpart = {"dp": (1 - xl) * 2 * NZ + z * 2 + c}
    xhpart = {"mp": y * 2 + 1 - xh}

    def at_z(zz):
        return {"dp": xl * 2 * NZ + zz * 2 + c}

    def at_mp(m):
        return {"mp": m}

    zup = at_z((z + 1) % NZ)
    zdown = at_z((z + NZ - 1) % NZ)

    def rcopy(src, dst, ssem, rsem, device):
        return pltpu.make_async_remote_copy(
            src_ref=src, dst_ref=dst, send_sem=ssem, recv_sem=rsem, device_id=device, device_id_type=MESH
        )

    loads = [
        pltpu.make_async_copy(src, dst, load_sem.at[i])
        for i, (src, dst) in enumerate(
            (
                (w6_hbm, w6_in),
                (wg_hbm, wg_in),
                (h6_hbm, h6),
                (hg_hbm, hg),
                (stu_hbm, stu),
                (p6_hbm, pt.at[pl.ds(0, 400)]),
                (pg_hbm, pt.at[pl.ds(400, 176)]),
                (r6_hbm, r6),
                (rg_hbm, rg),
            )
        )
    ]
    for load in loads:
        load.start()

    barrier = pltpu.get_barrier_semaphore()
    peers = [pair, xpart]
    peers += [at_z((z + o) % NZ) for o in range(1, NZ)]
    peers += [at_mp((mp + o) % 8) for o in range(1, 8)]
    for device in peers:
        pl.semaphore_signal(barrier, inc=1, device_id=device, device_id_type=MESH)

    def slot_of(block):
        plane, off = block
        pl_ = xl if plane == 0 else 1 - xl
        return pl_ * 2 * NZ + ((z + off + NZ) % NZ) * 2

    own = dp
    loads[0].wait()
    loads[1].wait()
    gath6[own] = jnp.zeros((112, 1664), BF16)
    gathg[own] = jnp.zeros((48, 768), BF16)
    gath6[own, 0:100, 0:1600] = w6_in[...]
    gathg[own, 0:44, :] = wg_in[...]

    pl.semaphore_wait(barrier, len(peers))

    def piece(p, slot):
        if p == 0:
            return gath6.at[slot, pl.ds(0, 64)]
        if p == 1:
            return gath6.at[slot, pl.ds(64, 48)]
        return gathg.at[slot]

    wtargets = (zup, zdown, xpart)
    pending = []

    def send_w(s, k, p):
        ref = piece(p, slot_of(SENDS[s][k]) + c)
        cp = rcopy(ref, ref, wsend_sem.at[p, 3 * s + k], wrecv_sem.at[p, 3 * s + k], wtargets[k])
        cp.start()
        pending.append(cp)

    def send_pair(unit, block, p):
        ref = piece(p, slot_of(block) + c)
        cp = rcopy(ref, ref, psend_sem.at[p, unit], precv_sem.at[p, unit], pair)
        cp.start()
        pending.append(cp)

    def wait_w(s, k, p):
        ref = piece(p, slot_of(RECVS[s][k]) + c)
        rcopy(ref, ref, wsend_sem.at[p, 3 * s + k], wrecv_sem.at[p, 3 * s + k], wtargets[k]).wait_recv()

    for p in range(3):
        for k in range(3):
            send_w(0, k, p)
    for p in range(3):
        send_pair(OWN, (0, 0), p)

    rows6[:, 1536:1664] = jnp.zeros((336, 128), BF16)
    loads[2].wait()
    loads[3].wait()
    for i in range(3):
        lane = lax.broadcasted_iota(jnp.int32, (112, 560), 1)
        pick = (keep_col[112 * i : 112 * i + 112, :] == lane).astype(F32).astype(BF16)
        rows6[112 * i : 112 * i + 112, 0:1600] = nn(pick, h6[i]).astype(BF16)
        rowsg[112 * i : 112 * i + 112, :] = nn(pick, hg[i]).astype(BF16)

    ysends = []

    def compute(unit, block):
        slot = slot_of(block)
        for p in range(3):
            ref = piece(p, slot + 1 - c)
            rcopy(ref, ref, psend_sem.at[p, unit], precv_sem.at[p, unit], pair).wait_recv()
        w = gath6[pl.ds(slot, 2)].reshape(224, 1664)
        part[pl.ds(slot, 2), 0:112, :] = nt(w, rows6[...]).astype(BF16).reshape(2, 112, 336)
        w = gathg[pl.ds(slot, 2)].reshape(96, 768)
        part[pl.ds(slot, 2), 112:160, :] = nt(w, rowsg[...]).astype(BF16).reshape(2, 48, 336)
        to_y = slot // 8
        u = (slot // 2) % 4
        o = (y - to_y + 3) % NY
        away = to_y != y

        def descriptor():
            ref = part.at[pl.ds(slot, 2)]
            return rcopy(ref, yrecv.at[o, u], ysend_sem.at[unit], yrecv_sem.at[o, u], at_mp(to_y * 2 + xh))

        @pl.when(away)
        def _():
            descriptor().start()

        ysends.append((away, descriptor))

    def heads():
        for load in loads[4:]:
            load.wait()
        outs[...] = nt(pt[...], stu[...])
        for l in range(11):
            pmat[128 * l : 128 * l + 128, :] = pt[:, 128 * l : 128 * l + 128].T
        for i in range(3):
            pos = lax.broadcasted_iota(jnp.int32, (560, 336), 0)
            col = lax.broadcasted_iota(jnp.int32, (560, 336), 1)
            clip = (col >= 112 * i) & (col < 112 * i + 112)
            pick = ((keep_row[...] == pos) & clip).astype(F32).astype(BF16)
            a = nn(r6[i], pick)
            b = nn(rg[i], pick)
            if i == 0:
                tgt[0:400, :] = a
                tgt[400:576, :] = b
            else:
                tgt[0:400, :] += a
                tgt[400:576, :] += b

    for s in range(STEPS):
        for p in range(3):
            for k in range(3):
                wait_w(s, k, p)
            if s + 1 < STEPS:
                for k in range(3):
                    send_w(s + 1, k, p)
            for k in range(3):
                send_pair(3 * s + k, RECVS[s][k], p)
            if s == 0:
                if p == 0:
                    compute(OWN, (0, 0))
                if p == 2:
                    heads()
            else:
                compute(3 * (s - 1) + p, RECVS[s - 1][p])
    for k in range(3):
        compute(3 * (STEPS - 1) + k, RECVS[STEPS - 1][k])

    def summed(u, cc):
        slot = y * 8 + u * 2 + cc
        total = part[slot].astype(F32)
        for o in range(3):
            total = total + yrecv[o, u, cc].astype(F32)
        return total

    def wait_y(u):
        for o in range(3):
            ref = yrecv.at[o, u]
            rcopy(ref, ref, ysend_sem.at[0], yrecv_sem.at[o, u], xhpart).wait_recv()

    for k in range(2):
        u = 2 * (1 - xh) + k
        wait_y(u)
        for cc in range(2):
            xsend[k, cc] = summed(u, cc).astype(BF16)
        cp = rcopy(xsend.at[k], xrecv.at[k], xh_sem.at[0, k], xh_sem.at[1, k], xhpart)
        cp.start()
        pending.append(cp)
    for k in range(2):
        u = 2 * xh + k
        wait_y(u)
        rcopy(xsend.at[k], xrecv.at[k], xh_sem.at[0, k], xh_sem.at[1, k], xhpart).wait_recv()
        for cc in range(2):
            total = summed(u, cc) + xrecv[k, cc].astype(F32)
            f = 100 * (2 * k + cc)
            tgt[f : f + 100, :] += total[0:100]
            f = 400 + 44 * (2 * k + cc)
            tgt[f : f + 44, :] += total[112:156]

    def sums(lo, hi):
        t = tgt[lo:hi, :]
        o = outs[lo:hi, :]
        return [
            jnp.sum(o * t, axis=0, keepdims=True),
            jnp.sum(o * o, axis=0, keepdims=True),
            jnp.sum(t * t, axis=0, keepdims=True),
        ]

    for i, row in enumerate(sums(0, 400) + sums(400, 576)):
        stats[mp, i : i + 1, :] = row
    for i in range(6, 8):
        stats[mp, i : i + 1, :] = jnp.zeros((1, 336), F32)
    st = []
    for o in range(1, 8):
        m = (mp + o) % 8
        cp = rcopy(stats.at[mp], stats.at[mp], st_sem.at[0, o], st_sem.at[1, mp], at_mp(m))
        cp.start()
        pending.append(cp)
    for o in range(1, 8):
        m = (mp + o) % 8
        rcopy(stats.at[m], stats.at[m], st_sem.at[0, o], st_sem.at[1, m], at_mp(m)).wait_recv()
    total = stats[0]
    for m in range(1, 8):
        total = total + stats[m]

    def gradient(lo, hi, i):
        norm_out = jnp.sqrt(total[i + 1 : i + 2] + norm_eps)
        norm_tar = jnp.sqrt(total[i + 2 : i + 3] + norm_eps)
        both = norm_out * norm_tar
        cosine = total[i : i + 1] / both
        a = -loss_scale / both
        b = loss_scale * cosine / (norm_out * norm_out)
        grad[lo:hi, :] = (tgt[lo:hi, :] * a + outs[lo:hi, :] * b).astype(BF16)
        return cosine

    cos6 = gradient(0, 400, 0)
    cosg = gradient(400, 576, 3)
    grad[576:640, :] = jnp.zeros((64, 336), BF16)
    loss_local = jnp.sum(2.0 - cos6 - cosg, axis=1, keepdims=True)
    lossz[z] = jnp.broadcast_to(loss_local, (8, 128))
    for o in range(1, NZ):
        zz = (z + o) % NZ
        cp = rcopy(lossz.at[z], lossz.at[z], l_sem.at[0, o], l_sem.at[1, z], at_z(zz))
        cp.start()
        pending.append(cp)

    order = [(z + o) % NZ for o in Z_ORDER] + [z]
    for kk in order:
        rows = grad[pl.ds(pl.multiple_of(kk * 80, 16), 80), :]
        g = nn(rows, stu[...]).astype(BF16)
        for q in range(3):
            gs[kk, q] = g[:, 384 * q : 384 * q + 384]
        gs[kk, 3, :, 0:256] = g[:, 1152:1408]
        gs[kk, 3, :, 256:384] = jnp.zeros((80, 128), BF16)
        cp = rcopy(gs.at[kk, pl.ds(2 * (1 - c), 2)], grecv.at[kk], g_sem.at[0, kk], g_sem.at[1, kk], pair)
        cp.start()
        pending.append(cp)

    for kk in order:
        rcopy(grecv.at[kk], grecv.at[kk], g_sem.at[0, kk], g_sem.at[1, kk], pair).wait_recv()
        gxs[kk] = (gs[kk, 2 * c + 1 - xl].astype(F32) + grecv[kk, 1 - xl].astype(F32)).astype(BF16)
        cp = rcopy(gxs.at[kk], gxr.at[kk], g_sem.at[2, kk], g_sem.at[3, kk], xpart)
        cp.start()
        pending.append(cp)

    def back_pair(t):
        yy = (y + t) % NY
        for j in range(2):
            rows = pmat[pl.ds(pl.multiple_of((yy * 2 + j) * 176, 16), 176), :]
            bsend[yy, j] = nn(rows, grad[0:576, :]).astype(BF16)
        if t:
            o = (3 - t) % NY
            cp = rcopy(bsend.at[yy], byr.at[o], b_sem.at[0, t], b_sem.at[1, o], at_mp(yy * 2 + xh))
            cp.start()
            pending.append(cp)

    for t in (2, 1, 3, 0):
        back_pair(t)

    gz_pending = []
    for kk in order:
        rcopy(gxr.at[kk], gxr.at[kk], g_sem.at[2, kk], g_sem.at[3, kk], xpart).wait_recv()
        v = gs[kk, 2 * c + xl].astype(F32) + grecv[kk, xl].astype(F32) + gxr[kk].astype(F32)
        gzs[kk] = v.astype(BF16)
        if kk is not z:
            cp = rcopy(gzs.at[kk], gzr.at[z], g_sem.at[4, kk], g_sem.at[5, z], at_z(kk))
            cp.start()
            pending.append(cp)

    for o in range(1, NZ):
        zz = (z + o) % NZ
        rcopy(lossz.at[zz], lossz.at[zz], l_sem.at[0, o], l_sem.at[1, zz], at_z(zz)).wait_recv()
    loss = lossz[0]
    for zz in range(1, NZ):
        loss = loss + lossz[zz]
    lossx[0] = loss
    cp = rcopy(lossx.at[0], lossx.at[1], l_sem.at[2, 0], l_sem.at[2, 1], xpart)
    cp.start()
    pending.append(cp)

    for o in range(3):
        rcopy(byr.at[o], byr.at[o], b_sem.at[0, 0], b_sem.at[1, o], xhpart).wait_recv()

    def back_sum(j):
        v = bsend[y, j].astype(F32)
        for o in range(3):
            v = v + byr[o, j].astype(F32)
        return v

    bxs[...] = back_sum(1 - xh).astype(BF16)
    bcp = rcopy(bxs, bxr, b_sem.at[2, 0], b_sem.at[2, 1], xhpart)
    bcp.start()
    pending.append(bcp)

    total = gzs[z].astype(F32)
    for o in range(1, NZ):
        zz = (z + o) % NZ
        rcopy(gzr.at[zz], gzr.at[zz], g_sem.at[4, zz], g_sem.at[5, zz], at_z(zz)).wait_recv()
        total = total + gzr[zz].astype(F32)
    q_own = 2 * c + xl
    q_x = 2 * c + 1 - xl
    ag[z, q_own] = (total * (head_scale / token_total)).astype(BF16)

    def ag_send(ref, ssem, rsem, device):
        cp = rcopy(ref, ref, ssem, rsem, device)
        cp.start()
        pending.append(cp)

    mine = ag.at[z, q_own]
    for o in Z_ORDER:
        zz = (z + o) % NZ
        ag_send(mine, agz_sem.at[0, zz], agz_sem.at[1, z], at_z(zz))
    ag_send(mine, agx_sem.at[0, z], agx_sem.at[1, z], xpart)
    ag_send(mine, agp_sem.at[0, z, xl], agp_sem.at[1, z, xl], pair)

    rcopy(lossx.at[0], lossx.at[1], l_sem.at[2, 0], l_sem.at[2, 1], xpart).wait_recv()
    lossc[0] = lossx[0] + lossx[1]
    cp = rcopy(lossc.at[0], lossc.at[1], l_sem.at[3, 0], l_sem.at[3, 1], pair)
    cp.start()
    pending.append(cp)
    bcp.wait_recv()
    bfin[...] = back_sum(xh) + bxr[...].astype(F32)
    back_store = pltpu.make_async_copy(bfin, back_out, out_sem.at[8])
    back_store.start()

    zs = [z] + [(z + o) % NZ for o in (1, 7, 2, 6, 3, 5, 4)]
    for zz in zs:
        if zz is not z:
            ref = ag.at[zz, q_own]
            rcopy(ref, ref, agz_sem.at[0, zz], agz_sem.at[1, zz], at_z(zz)).wait_recv()
            ag_send(ref, agx_sem.at[0, zz], agx_sem.at[1, zz], xpart)
            ag_send(ref, agp_sem.at[0, zz, xl], agp_sem.at[1, zz, xl], pair)
    for zz in zs:
        ref = ag.at[zz, q_x]
        rcopy(ref, ref, agx_sem.at[0, zz], agx_sem.at[1, zz], xpart).wait_recv()
        ag_send(ref, agp_sem.at[0, zz, 1 - xl], agp_sem.at[1, zz, 1 - xl], pair)

    rcopy(lossc.at[0], lossc.at[1], l_sem.at[3, 0], l_sem.at[3, 1], pair).wait_recv()
    lossv[...] = (lossc[0] + lossc[1]) / token_total
    loss_store = pltpu.make_async_copy(lossv, loss_out, out_sem.at[9])
    loss_store.start()

    stores = [back_store, loss_store]
    for zz in range(NZ):
        for x in range(2):
            ref = ag.at[zz, 2 * (1 - c) + x]
            rcopy(ref, ref, agp_sem.at[0, zz, x], agp_sem.at[1, zz, x], pair).wait_recv()
        n = 80 if zz < 7 else 16
        for q in range(4):
            w = 384 if q < 3 else 256
            fout[80 * zz : 80 * zz + n, 384 * q : 384 * q + w] = ag[zz, q, 0:n, 0:w].astype(F32)
        src = fout.at[pl.ds(80 * zz, n)]
        dst = gp6_out.at[pl.ds(80 * zz, n)] if zz < 5 else gpg_out.at[pl.ds(80 * zz - 400, n)]
        cp = pltpu.make_async_copy(src, dst, out_sem.at[zz])
        cp.start()
        stores.append(cp)

    for away, descriptor in ysends:

        @pl.when(away)
        def _(descriptor=descriptor):
            descriptor().wait_send()

    for cp in pending:
        cp.wait_send()
    for cp in stores:
        cp.wait()


def local(
    student_feats,
    keep_index,
    hidden_six,
    resid_six,
    down_six,
    hidden_giant,
    resid_giant,
    down_giant,
    proj_six,
    proj_giant,
):
    token_total = 336 * 32
    dma = pltpu.SemaphoreType.DMA
    hbm = pl.BlockSpec(memory_space=pl.ANY)
    vmem = pl.BlockSpec(memory_space=pltpu.VMEM)
    scratch = [
        pltpu.VMEM((100, 1600), BF16),
        pltpu.VMEM((44, 768), BF16),
        pltpu.VMEM((32, 112, 1664), BF16),
        pltpu.VMEM((32, 48, 768), BF16),
        pltpu.VMEM((3, 560, 1600), BF16),
        pltpu.VMEM((3, 560, 768), BF16),
        pltpu.VMEM((3, 400, 560), BF16),
        pltpu.VMEM((3, 176, 560), BF16),
        pltpu.VMEM((336, 1664), BF16),
        pltpu.VMEM((336, 768), BF16),
        pltpu.VMEM((336, 1408), BF16),
        pltpu.VMEM((576, 1408), BF16),
        pltpu.VMEM((1408, 576), BF16),
        pltpu.VMEM((32, 160, 336), BF16),
        pltpu.VMEM((3, 4, 2, 160, 336), BF16),
        pltpu.VMEM((2, 2, 160, 336), BF16),
        pltpu.VMEM((2, 2, 160, 336), BF16),
        pltpu.VMEM((576, 336), F32),
        pltpu.VMEM((576, 336), F32),
        pltpu.VMEM((8, 8, 336), F32),
        pltpu.VMEM((640, 336), BF16),
        pltpu.VMEM((NZ, 4, 80, 384), BF16),
        pltpu.VMEM((NZ, 2, 80, 384), BF16),
        pltpu.VMEM((NZ, 80, 384), BF16),
        pltpu.VMEM((NZ, 80, 384), BF16),
        pltpu.VMEM((NZ, 80, 384), BF16),
        pltpu.VMEM((NZ, 80, 384), BF16),
        pltpu.VMEM((NZ, 4, 80, 384), BF16),
        pltpu.VMEM((576, 1408), F32),
        pltpu.VMEM((NY, 2, 176, 336), BF16),
        pltpu.VMEM((3, 2, 176, 336), BF16),
        pltpu.VMEM((176, 336), BF16),
        pltpu.VMEM((176, 336), BF16),
        pltpu.VMEM((176, 336), F32),
        pltpu.VMEM((NZ, 8, 128), F32),
        pltpu.VMEM((2, 8, 128), F32),
        pltpu.VMEM((2, 8, 128), F32),
        pltpu.VMEM((8, 128), F32),
        dma((9,)),
        dma((3, 15)),
        dma((3, 15)),
        dma((3, 16)),
        dma((3, 16)),
        dma((16,)),
        dma((3, 4)),
        dma((2, 2)),
        dma((2, 8)),
        dma((6, 8)),
        dma((2, 8)),
        dma((2, 8)),
        dma((2, 8, 2)),
        dma((3, 4)),
        dma((4, 8)),
        dma((10,)),
    ]
    gp6, gpg, back, loss = pl.pallas_call(
        functools.partial(kernel, token_total),
        out_shape=(
            jax.ShapeDtypeStruct((400, 1408), F32),
            jax.ShapeDtypeStruct((176, 1408), F32),
            jax.ShapeDtypeStruct((176, 336), F32),
            jax.ShapeDtypeStruct((8, 128), F32),
        ),
        in_specs=[vmem, vmem] + [hbm] * 9,
        out_specs=(hbm, hbm, hbm, hbm),
        scratch_shapes=scratch,
        compiler_params=pltpu.CompilerParams(
            collective_id=0, has_side_effects=True, vmem_limit_bytes=62 * 1024 * 1024
        ),
        cost_estimate=pl.CostEstimate(flops=6_000_000_000, bytes_accessed=20_000_000, transcendentals=0),
    )(
        keep_index.reshape(1, 336),
        keep_index.reshape(336, 1),
        student_feats.reshape(336, 1408),
        hidden_six,
        resid_six.transpose(0, 2, 1),
        down_six.T,
        hidden_giant,
        resid_giant.transpose(0, 2, 1),
        down_giant.T,
        proj_six.T,
        proj_giant.T,
    )
    grad_student = back.reshape(176, 3, 112).transpose(1, 2, 0)
    return (grad_student, gp6.T, gpg.T, loss[0, 0])


def solution(mesh):
    return jax.shard_map(
        local,
        mesh=mesh,
        in_specs=(
            P("dp", None, None),
            P("dp", None),
            P("dp", None, "mp"),
            P("dp", None, "mp"),
            P("mp", "dp"),
            P("dp", None, "mp"),
            P("dp", None, "mp"),
            P("mp", "dp"),
            P(None, "mp"),
            P(None, "mp"),
        ),
        out_specs=(P("dp", None, "mp"), P(None, "mp"), P(None, "mp"), P()),
        check_vma=False,
    )
```

time: 690 us -> 177 us (0.26)
  waiting for transfers between devices: 470 us -> 0 us
  Pallas kernels: 0 us -> 166 us
  blocking collectives: 94.4 us -> 0 us
  local copies, waits for them, and re-layouts: 72.7 us -> 10.1 us
  matrix products: 26.2 us -> 0 us
  between operations: 16 us -> 0.65 us
  other arithmetic: 8.82 us -> 0 us
    reduce_scatter x3 -> x0, waiting for transfers between devices: 182 us -> none  [the longest x1 81.7 us: local(): lax.psum_scatter(part_six.astype(jnp.bfloat16), 'mp', scatter_dimension=1...]
    psum x1 -> x0, waiting for transfers between devices: 168 us -> none  [local(): lax.psum((head_six, head_giant, loss_local), 'dp')]
    pallas_call x0 -> x1, Pallas kernels: none -> 166 us  [local(): pl.pallas_call(functools.partial(kernel, token_total), out_shape=(jax.Sha...]
    all_gather x2 -> x0, waiting for transfers between devices: 119 us -> none  [the longest x1 62.9 us: local(): lax.all_gather(down_giant, 'dp', axis=1, tiled=True)]
    psum x2 -> x0, blocking collectives: 94.4 us -> none  [the longest x1 62.2 us: local(): lax.psum((head_six, head_giant, loss_local), 'dp')]
    gather x7 -> x0, local copies, waits for them, and re-layouts: 42.7 us -> none  [select_kept(): chosen = jnp.take_along_axis(values, keep_index[:, :, None], axis=1)]
    dot_general x8 -> x0, matrix products: 26.2 us -> none  [the longest x1 10.2 us: local(): jnp.dot(rows_six, lax.all_gather(down_six, 'dp', axis=1, tiled=True), pre...]
    unnamed x31 -> x5, local copies, waits for them, and re-layouts: 26.8 us -> 4.91 us
  transfers between devices with their start and end apart: 6 -> 0, of which waited for: 6 -> 0; matrix products, arithmetic and copies ran while one was open for 13% -> 0% of each run, Pallas kernels for 0% -> 0%
where the time goes in v1:
time: 177 us
  Pallas kernels  166 us (94%)
  local copies, waits for them, and re-layouts  10.1 us (6%)
    pallas_call x1, Pallas kernels, local(): pl.pallas_call(functools.partial(kernel, token_total), out_shape=(jax.Sha...  166 us
    unnamed x5, local copies, waits for them, and re-layouts  4.91 us

profile of v1, /device:TPU:1, one launch (start us, length us, event | category | flops | bytes accessed | tf_op | source)
XLA Modules:
  0.0 176.9 jit_solution(16575562510733539227)
XLA Ops:
  0.6 1.3 reshape.20.keep_row
  2.0 1.5 reshape.24.keep_col
  3.5 166.1 %shard_map.129 = (f32[400,1408]{1,0:T(8,128)}, f32[176,1408]{1,0:T(8,128)}, f32[176,336]{1,0:T(8,128)}, f32[8,128]{1,0:T(8,128)}) custom-call(s32[1,336]{1,0:T(1,128)} %reshape.20.keep_row, s32[336,1]{1,0:T(8,128)} %reshape.24.keep_col, bf16[336,1408]{1,0:T(8,128)(2,1)} %bitcast.16, bf16[3,560,1600]{2,1,0:T(8,128)(2,1)} %h6_hbm.1, ...), custom_call_target="tpu_custom_call" | custom-call | flops 6000000000 | bytes 20000000 | tf_op jit(solution)/shard_map/pallas_call | solution.py:585
  169.6 1.2 slice.3
  170.8 1.2 reshape.23
  171.9 0.7 copy.16
  172.7 0.0 copy-start
  172.7 3.2 %copy.19 = f32[1408,400]{0,1:T(8,128)} copy(f32[1408,400]{0,1:T(8,128)} %bitcast.11) | data formatting | bytes 4505600
  175.9 0.0 copy-done
  175.9 0.9 copy.20
Async XLA Ops:
  172.7 3.2 %copy-start = (f32[176,1408]{1,0:T(8,128)S(1)}, f32[176,1408]{1,0:T(8,128)}, u32[]{:S(2)}) copy-start(f32[176,1408]{1,0:T(8,128)} %get-tuple-element.10) | copy-start | bytes 2973700

commit v2 on v1

--- a/solution.py
+++ b/solution.py
@@ -46,8 +46,7 @@
 
 def kernel(
     token_total,
-    keep_row,
-    keep_col,
+    keep,
     stu_hbm,
     h6_hbm,
     r6_hbm,
@@ -78,6 +77,8 @@
     yrecv,
     xsend,
     xrecv,
+    wpad,
+    yrel,
     tgt,
     outs,
     stats,
@@ -89,7 +90,6 @@
     gzs,
     gzr,
     ag,
-    fout,
     bsend,
     byr,
     bxs,
@@ -98,7 +98,6 @@
     lossz,
     lossx,
     lossc,
-    lossv,
     load_sem,
     wsend_sem,
     wrecv_sem,
@@ -106,6 +105,7 @@
     precv_sem,
     ysend_sem,
     yrecv_sem,
+    yrel_sem,
     xh_sem,
     st_sem,
     g_sem,
@@ -135,6 +135,8 @@
         return {"mp": m}
 
     zup = at_z((z + 1) % NZ)
+    yup = at_mp(((y + 1) % NY) * 2 + xh)
+    ydown = at_mp(((y + NY - 1) % NY) * 2 + xh)
     zdown = at_z((z + NZ - 1) % NZ)
 
     def rcopy(src, dst, ssem, rsem, device):
@@ -177,9 +179,10 @@
     loads[0].wait()
     loads[1].wait()
     gath6[own] = jnp.zeros((112, 1664), BF16)
-    gathg[own] = jnp.zeros((48, 768), BF16)
     gath6[own, 0:100, 0:1600] = w6_in[...]
-    gathg[own, 0:44, :] = wg_in[...]
+    wpad[0:4, :] = jnp.zeros((4, 768), F32)
+    wpad[4:48, :] = wg_in[...].astype(F32)
+    gathg[own] = wpad[...].astype(BF16)
 
     pl.semaphore_wait(barrier, len(peers))
 
@@ -215,60 +218,100 @@
     for p in range(3):
         send_pair(OWN, (0, 0), p)
 
+    def column(row):
+        a = lax.broadcasted_iota(jnp.int32, (112, 112), 0)
+        b = lax.broadcasted_iota(jnp.int32, (112, 112), 1)
+        return jnp.sum(jnp.where(a == b, row.astype(F32), 0.0), axis=1, keepdims=True)
+
     rows6[:, 1536:1664] = jnp.zeros((336, 128), BF16)
+    def pick_rows(i):
+        lane = lax.broadcasted_iota(jnp.int32, (112, 560), 1).astype(F32)
+        pick = (column(keep[i : i + 1, :]) == lane).astype(F32).astype(BF16)
+        rows6[112 * i : 112 * i + 112, 0:1600] = nn(pick, h6[i]).astype(BF16)
+        rowsg[112 * i : 112 * i + 112, :] = nn(pick, hg[i]).astype(BF16)
+
     loads[2].wait()
     loads[3].wait()
-    for i in range(3):
-        lane = lax.broadcasted_iota(jnp.int32, (112, 560), 1)
-        pick = (keep_col[112 * i : 112 * i + 112, :] == lane).astype(F32).astype(BF16)
-        rows6[112 * i : 112 * i + 112, 0:1600] = nn(pick, h6[i]).astype(BF16)
-        rowsg[112 * i : 112 * i + 112, :] = nn(pick, hg[i]).astype(BF16)
+    pick_rows(0)
+    pick_rows(1)
 
     ysends = []
+    relays = []
+    relayed = 0
 
     def compute(unit, block):
         slot = slot_of(block)
         for p in range(3):
             ref = piece(p, slot + 1 - c)
             rcopy(ref, ref, psend_sem.at[p, unit], precv_sem.at[p, unit], pair).wait_recv()
-        w = gath6[pl.ds(slot, 2)].reshape(224, 1664)
-        part[pl.ds(slot, 2), 0:112, :] = nt(w, rows6[...]).astype(BF16).reshape(2, 112, 336)
-        w = gathg[pl.ds(slot, 2)].reshape(96, 768)
-        part[pl.ds(slot, 2), 112:160, :] = nt(w, rowsg[...]).astype(BF16).reshape(2, 48, 336)
-        to_y = slot // 8
+        six = nt(gath6[pl.ds(slot, 2)].reshape(224, 1664), rows6[...])
+        giant = nt(gathg[pl.ds(slot, 2)].reshape(96, 768), rowsg[...])
+        for cc in range(2):
+            a = six[112 * cc : 112 * cc + 112]
+            b = giant[48 * cc : 48 * cc + 48]
+            part[slot + cc, 0:96, :] = a[0:96].astype(BF16)
+            part[slot + cc, 96:112, :] = (a[96:112] + b[0:16]).astype(BF16)
+            part[slot + cc, 112:144, :] = b[16:48].astype(BF16)
+        role = (y - slot // 8 + NY) % NY
         u = (slot // 2) % 4
-        o = (y - to_y + 3) % NY
-        away = to_y != y
-
-        def descriptor():
-            ref = part.at[pl.ds(slot, 2)]
-            return rcopy(ref, yrecv.at[o, u], ysend_sem.at[unit], yrecv_sem.at[o, u], at_mp(to_y * 2 + xh))
-
-        @pl.when(away)
-        def _():
-            descriptor().start()
-
-        ysends.append((away, descriptor))
-
-    def heads():
-        for load in loads[4:]:
-            load.wait()
-        outs[...] = nt(pt[...], stu[...])
-        for l in range(11):
+
+        def send(cond, src, dst, ssem, rsem, device):
+            @pl.when(cond)
+            def _():
+                rcopy(src, dst, ssem, rsem, device).start()
+
+            ysends.append((cond, lambda: rcopy(src, dst, ssem, rsem, device)))
+
+        first, second = part.at[slot], part.at[slot + 1]
+        send(role == 2, first, yrel.at[unit], ysend_sem.at[unit, 0], yrel_sem.at[unit], ydown)
+        send(role == 2, second, yrel.at[unit], ysend_sem.at[unit, 1], yrel_sem.at[unit], yup)
+        send(role == 1, second, yrecv.at[0, u, 1], ysend_sem.at[unit, 0], yrecv_sem.at[0, u, 1], ydown)
+        send(role == 3, first, yrecv.at[1, u, 0], ysend_sem.at[unit, 0], yrecv_sem.at[1, u, 0], yup)
+
+        def relay():
+            for want, cc, side, device in ((1, 0, 0, ydown), (3, 1, 1, yup)):
+                src, dst = part.at[slot + cc], yrecv.at[side, u, cc]
+                ssem, rsem = ysend_sem.at[unit, 1], yrecv_sem.at[side, u, cc]
+
+                @pl.when(role == want)
+                def _(cc=cc, src=src, dst=dst, ssem=ssem, rsem=rsem, device=device):
+                    ref = yrel.at[unit]
+                    rcopy(ref, ref, ssem, yrel_sem.at[unit], device).wait_recv()
+                    part[slot + cc] = (part[slot + cc].astype(F32) + yrel[unit].astype(F32)).astype(BF16)
+                    rcopy(src, dst, ssem, rsem, device).start()
+
+                ysends.append((role == want, lambda src=src, dst=dst, ssem=ssem, rsem=rsem, device=device: rcopy(src, dst, ssem, rsem, device)))
+
+        relays.append(relay)
+
+    def head_out(i):
+        if i == 0:
+            for load in loads[4:]:
+                load.wait()
+        outs[192 * i : 192 * i + 192, :] = nt(pt[192 * i : 192 * i + 192, :], stu[...])
+
+    def turn_heads(lo, hi):
+        for l in range(lo, hi):
             pmat[128 * l : 128 * l + 128, :] = pt[:, 128 * l : 128 * l + 128].T
-        for i in range(3):
-            pos = lax.broadcasted_iota(jnp.int32, (560, 336), 0)
-            col = lax.broadcasted_iota(jnp.int32, (560, 336), 1)
-            clip = (col >= 112 * i) & (col < 112 * i + 112)
-            pick = ((keep_row[...] == pos) & clip).astype(F32).astype(BF16)
-            a = nn(r6[i], pick)
-            b = nn(rg[i], pick)
-            if i == 0:
-                tgt[0:400, :] = a
-                tgt[400:576, :] = b
-            else:
-                tgt[0:400, :] += a
-                tgt[400:576, :] += b
+
+    def residuals(i):
+        row = jnp.concatenate([keep[j : j + 1, :] for j in range(3)], axis=1)
+        pos = lax.broadcasted_iota(jnp.int32, (560, 336), 0)
+        col = lax.broadcasted_iota(jnp.int32, (560, 336), 1)
+        clip = (col >= 112 * i) & (col < 112 * i + 112)
+        pick = ((row == pos) & clip).astype(F32).astype(BF16)
+        a = nn(r6[i], pick)
+        b = nn(rg[i], pick)
+        if i == 0:
+            tgt[0:400, :] = a
+            tgt[400:576, :] = b
+        else:
+            tgt[0:400, :] += a
+            tgt[400:576, :] += b
+
+    work = [functools.partial(head_out, i) for i in range(3)]
+    work += [functools.partial(residuals, i) for i in range(3)]
+    work += [functools.partial(turn_heads, 0, 6), functools.partial(turn_heads, 6, 11)]
 
     for s in range(STEPS):
         for p in range(3):
@@ -279,46 +322,66 @@
                     send_w(s + 1, k, p)
             for k in range(3):
                 send_pair(3 * s + k, RECVS[s][k], p)
-            if s == 0:
-                if p == 0:
-                    compute(OWN, (0, 0))
-                if p == 2:
-                    heads()
-            else:
+            if s > 0:
                 compute(3 * (s - 1) + p, RECVS[s - 1][p])
+            elif p == 0:
+                pick_rows(2)
+            elif p == 1:
+                compute(OWN, (0, 0))
+            if p != (1 if s == 0 else 2) and s + p > 0 and work:
+                work.pop(0)()
+            while len(relays) - relayed > 2:
+                relays[relayed]()
+                relayed += 1
+    while work:
+        work.pop(0)()
+
+    def summed(u, cc):
+        total = part[y * 8 + u * 2 + cc].astype(F32)
+        for side in range(2):
+            total = total + yrecv[side, u, cc].astype(F32)
+        return total
+
+    def wait_y(u):
+        for side in range(2):
+            for cc in range(2):
+                ref = yrecv.at[side, u, cc]
+                rcopy(ref, ref, ysend_sem.at[0, 0], yrecv_sem.at[side, u, cc], xhpart).wait_recv()
+
+    def xh_copy(k):
+        return rcopy(xsend.at[k], xrecv.at[k], xh_sem.at[0, k], xh_sem.at[1, k], xhpart)
+
+    def exchange():
+        for k in range(2):
+            u = 2 * (1 - xh) + k
+            wait_y(u)
+            for cc in range(2):
+                xsend[k, cc] = summed(u, cc).astype(BF16)
+            xh_copy(k).start()
+
+    def targets():
+        for k in range(2):
+            u = 2 * xh + k
+            wait_y(u)
+            xh_copy(k).wait_recv()
+            for cc in range(2):
+                total = summed(u, cc) + xrecv[k, cc].astype(F32)
+                f = 100 * (2 * k + cc)
+                tgt[f : f + 100, :] += total[0:100]
+                f = 400 + 44 * (2 * k + cc)
+                tgt[f : f + 44, :] += total[100:144]
+
+    early = y // 2 == xl
+    for i in range(relayed, len(relays)):
+        relays[i]()
+    relayed = len(relays)
+    pl.when(early)(exchange)
     for k in range(3):
         compute(3 * (STEPS - 1) + k, RECVS[STEPS - 1][k])
-
-    def summed(u, cc):
-        slot = y * 8 + u * 2 + cc
-        total = part[slot].astype(F32)
-        for o in range(3):
-            total = total + yrecv[o, u, cc].astype(F32)
-        return total
-
-    def wait_y(u):
-        for o in range(3):
-            ref = yrecv.at[o, u]
-            rcopy(ref, ref, ysend_sem.at[0], yrecv_sem.at[o, u], xhpart).wait_recv()
-
-    for k in range(2):
-        u = 2 * (1 - xh) + k
-        wait_y(u)
-        for cc in range(2):
-            xsend[k, cc] = summed(u, cc).astype(BF16)
-        cp = rcopy(xsend.at[k], xrecv.at[k], xh_sem.at[0, k], xh_sem.at[1, k], xhpart)
-        cp.start()
-        pending.append(cp)
-    for k in range(2):
-        u = 2 * xh + k
-        wait_y(u)
-        rcopy(xsend.at[k], xrecv.at[k], xh_sem.at[0, k], xh_sem.at[1, k], xhpart).wait_recv()
-        for cc in range(2):
-            total = summed(u, cc) + xrecv[k, cc].astype(F32)
-            f = 100 * (2 * k + cc)
-            tgt[f : f + 100, :] += total[0:100]
-            f = 400 + 44 * (2 * k + cc)
-            tgt[f : f + 44, :] += total[112:156]
+    for i in range(relayed, len(relays)):
+        relays[i]()
+    pl.when(jnp.logical_not(early))(exchange)
+    targets()
 
     def sums(lo, hi):
         t = tgt[lo:hi, :]
@@ -462,8 +525,10 @@
     cp.start()
     pending.append(cp)
     bcp.wait_recv()
-    bfin[...] = back_sum(xh) + bxr[...].astype(F32)
-    back_store = pltpu.make_async_copy(bfin, back_out, out_sem.at[8])
+    v = back_sum(xh) + bxr[...].astype(F32)
+    for i in range(3):
+        bfin[i] = v[:, 112 * i : 112 * i + 112]
+    back_store = pltpu.make_async_copy(bfin, back_out, out_sem.at[8, 0])
     back_store.start()
 
     zs = [z] + [(z + o) % NZ for o in (1, 7, 2, 6, 3, 5, 4)]
@@ -479,24 +544,22 @@
         ag_send(ref, agp_sem.at[0, zz, 1 - xl], agp_sem.at[1, zz, 1 - xl], pair)
 
     rcopy(lossc.at[0], lossc.at[1], l_sem.at[3, 0], l_sem.at[3, 1], pair).wait_recv()
-    lossv[...] = (lossc[0] + lossc[1]) / token_total
-    loss_store = pltpu.make_async_copy(lossv, loss_out, out_sem.at[9])
-    loss_store.start()
-
-    stores = [back_store, loss_store]
+    loss_out[...] = (lossc[0, 0:1, 0:1] + lossc[1, 0:1, 0:1]) / token_total
+
+    stores = [back_store]
     for zz in range(NZ):
         for x in range(2):
             ref = ag.at[zz, 2 * (1 - c) + x]
             rcopy(ref, ref, agp_sem.at[0, zz, x], agp_sem.at[1, zz, x], pair).wait_recv()
         n = 80 if zz < 7 else 16
+        out, lo = (gp6_out, 80 * zz) if zz < 5 else (gpg_out, 80 * zz - 400)
         for q in range(4):
             w = 384 if q < 3 else 256
-            fout[80 * zz : 80 * zz + n, 384 * q : 384 * q + w] = ag[zz, q, 0:n, 0:w].astype(F32)
-        src = fout.at[pl.ds(80 * zz, n)]
-        dst = gp6_out.at[pl.ds(80 * zz, n)] if zz < 5 else gpg_out.at[pl.ds(80 * zz - 400, n)]
-        cp = pltpu.make_async_copy(src, dst, out_sem.at[zz])
-        cp.start()
-        stores.append(cp)
+            cp = pltpu.make_async_copy(
+                ag.at[zz, q, pl.ds(0, n), pl.ds(0, w)], out.at[pl.ds(lo, n), pl.ds(384 * q, w)], out_sem.at[zz, q]
+            )
+            cp.start()
+            stores.append(cp)
 
     for away, descriptor in ysends:
 
@@ -504,6 +567,8 @@
         def _(descriptor=descriptor):
             descriptor().wait_send()
 
+    for k in range(2):
+        xh_copy(k).wait_send()
     for cp in pending:
         cp.wait_send()
     for cp in stores:
@@ -540,10 +605,12 @@
         pltpu.VMEM((336, 1408), BF16),
         pltpu.VMEM((576, 1408), BF16),
         pltpu.VMEM((1408, 576), BF16),
-        pltpu.VMEM((32, 160, 336), BF16),
-        pltpu.VMEM((3, 4, 2, 160, 336), BF16),
-        pltpu.VMEM((2, 2, 160, 336), BF16),
-        pltpu.VMEM((2, 2, 160, 336), BF16),
+        pltpu.VMEM((32, 144, 336), BF16),
+        pltpu.VMEM((2, 4, 2, 144, 336), BF16),
+        pltpu.VMEM((2, 2, 144, 336), BF16),
+        pltpu.VMEM((2, 2, 144, 336), BF16),
+        pltpu.VMEM((48, 768), F32),
+        pltpu.VMEM((16, 144, 336), BF16),
         pltpu.VMEM((576, 336), F32),
         pltpu.VMEM((576, 336), F32),
         pltpu.VMEM((8, 8, 336), F32),
@@ -555,23 +622,22 @@
         pltpu.VMEM((NZ, 80, 384), BF16),
         pltpu.VMEM((NZ, 80, 384), BF16),
         pltpu.VMEM((NZ, 4, 80, 384), BF16),
-        pltpu.VMEM((576, 1408), F32),
         pltpu.VMEM((NY, 2, 176, 336), BF16),
         pltpu.VMEM((3, 2, 176, 336), BF16),
         pltpu.VMEM((176, 336), BF16),
         pltpu.VMEM((176, 336), BF16),
-        pltpu.VMEM((176, 336), F32),
+        pltpu.VMEM((3, 176, 112), F32),
         pltpu.VMEM((NZ, 8, 128), F32),
         pltpu.VMEM((2, 8, 128), F32),
         pltpu.VMEM((2, 8, 128), F32),
-        pltpu.VMEM((8, 128), F32),
         dma((9,)),
         dma((3, 15)),
         dma((3, 15)),
         dma((3, 16)),
         dma((3, 16)),
+        dma((16, 2)),
+        dma((2, 4, 2)),
         dma((16,)),
-        dma((3, 4)),
         dma((2, 2)),
         dma((2, 8)),
         dma((6, 8)),
@@ -580,26 +646,25 @@
         dma((2, 8, 2)),
         dma((3, 4)),
         dma((4, 8)),
-        dma((10,)),
+        dma((9, 4)),
     ]
     gp6, gpg, back, loss = pl.pallas_call(
         functools.partial(kernel, token_total),
         out_shape=(
-            jax.ShapeDtypeStruct((400, 1408), F32),
-            jax.ShapeDtypeStruct((176, 1408), F32),
-            jax.ShapeDtypeStruct((176, 336), F32),
-            jax.ShapeDtypeStruct((8, 128), F32),
+            jax.ShapeDtypeStruct((400, 1408), BF16),
+            jax.ShapeDtypeStruct((176, 1408), BF16),
+            jax.ShapeDtypeStruct((3, 176, 112), F32),
+            jax.ShapeDtypeStruct((1, 1), F32),
         ),
-        in_specs=[vmem, vmem] + [hbm] * 9,
-        out_specs=(hbm, hbm, hbm, hbm),
+        in_specs=[vmem] + [hbm] * 9,
+        out_specs=(hbm, hbm, hbm, vmem),
         scratch_shapes=scratch,
         compiler_params=pltpu.CompilerParams(
             collective_id=0, has_side_effects=True, vmem_limit_bytes=62 * 1024 * 1024
         ),
         cost_estimate=pl.CostEstimate(flops=6_000_000_000, bytes_accessed=20_000_000, transcendentals=0),
     )(
-        keep_index.reshape(1, 336),
-        keep_index.reshape(336, 1),
+        keep_index,
         student_feats.reshape(336, 1408),
         hidden_six,
         resid_six.transpose(0, 2, 1),
@@ -610,8 +675,7 @@
         proj_six.T,
         proj_giant.T,
     )
-    grad_student = back.reshape(176, 3, 112).transpose(1, 2, 0)
-    return (grad_student, gp6.T, gpg.T, loss[0, 0])
+    return (back.transpose(0, 2, 1), gp6.astype(F32).T, gpg.astype(F32).T, loss.reshape(()))
 
 
 def solution(mesh):

time: 177 us -> 152 us (0.86)
  Pallas kernels: 166 us -> 144 us
  local copies, waits for them, and re-layouts: 10.1 us -> 0.71 us
  other arithmetic: 0 us -> 3.85 us
  between operations: 0.65 us -> 2.43 us
    pallas_call x1, Pallas kernels: 166 us -> 144 us  [local(): pl.pallas_call(functools.partial(kernel, token_total), out_shape=(jax.Sha...]
    unnamed x5, local copies, waits for them, and re-layouts: 4.91 us -> 0.71 us
    reshape x3 -> x0, local copies, waits for them, and re-layouts: 4.02 us -> none  [the longest x1 1.54 us: local(): keep_index.reshape(336, 1)]
    transpose x0 -> x2, other arithmetic: none -> 3.85 us  [the longest x1 2.84 us: local(): gp6.astype(F32)]
where the time goes in v2:
time: 152 us; the launch traced here: 151 us
  Pallas kernels  144 us (95%)
  other arithmetic  3.85 us (3%)
  between operations  2.43 us (2%)
    pallas_call x1, Pallas kernels, local(): pl.pallas_call(functools.partial(kernel, token_total), out_shape=(jax.Sha...  144 us

profile of v2, /device:TPU:1, one launch (start us, length us, event | category | flops | bytes accessed | tf_op | source)
XLA Modules:
  0.0 150.8 jit_solution(16060822212186889741)
XLA Ops:
  0.6 143.8 %shard_map.129 = (bf16[400,1408]{1,0:T(8,128)(2,1)}, bf16[176,1408]{1,0:T(8,128)(2,1)}, f32[3,176,112]{2,1,0:T(8,128)}, f32[1,1]{1,0:T(1,128)}) custom-call(s32[3,112]{1,0:T(4,128)} %keep.1, bf16[336,1408]{1,0:T(8,128)(2,1)} %bitcast.16, bf16[3,560,1600]{2,1,0:T(8,128)(2,1)} %h6_hbm.1, bf16[3,400,560]{2,1,0:T(8,128)(2,1)} %bitcast.14, ...), custom_call_target="tpu_custom_call" | custom-call | flops 6000000000 | bytes 20000000 | tf_op jit(solution)/shard_map/pallas_call | solution.py:651
  144.5 0.0 copy-start
  144.5 0.0 copy-start.1
  144.5 2.8 %convert_bitcast_fusion = f32[1408,400]{0,1:T(8,128)} fusion(bf16[400,1408]{1,0:T(8,128)(2,1)} %get-tuple-element.9), kind=kLoop, calls=%fused_computation | loop fusion | flops 563200 | bytes 3379200 | tf_op jit(solution)/shard_map/transpose | solution.py:678
  147.3 0.0 copy-done
  147.3 1.0 convert_bitcast_fusion.1
  148.4 0.0 copy-done.1
  148.4 0.7 copy.16
Async XLA Ops:
  144.5 2.9 %copy-start = (bf16[176,1408]{1,0:T(8,128)(2,1)S(1)}, bf16[176,1408]{1,0:T(8,128)(2,1)}, u32[]{:S(2)}) copy-start(bf16[176,1408]{1,0:T(8,128)(2,1)} %get-tuple-element.10) | copy-start | bytes 1486852
  144.5 3.9 %copy-start.1 = (f32[3,176,112]{2,1,0:T(8,128)S(1)}, f32[3,176,112]{2,1,0:T(8,128)}, u32[]{:S(2)}) copy-start(f32[3,176,112]{2,1,0:T(8,128)} %get-tuple-element.8) | copy-start | bytes 709636

commit v3 on v2

--- a/solution.py
+++ b/solution.py
@@ -90,6 +90,7 @@
     gzs,
     gzr,
     ag,
+    fout,
     bsend,
     byr,
     bxs,
@@ -144,6 +145,13 @@
             src_ref=src, dst_ref=dst, send_sem=ssem, recv_sem=rsem, device_id=device, device_id_type=MESH
         )
 
+    barrier = pltpu.get_barrier_semaphore()
+    peers = [pair, xpart]
+    peers += [at_z((z + o) % NZ) for o in range(1, NZ)]
+    peers += [at_mp((mp + o) % 8) for o in range(1, 8)]
+    for device in peers:
+        pl.semaphore_signal(barrier, inc=1, device_id=device, device_id_type=MESH)
+
     loads = [
         pltpu.make_async_copy(src, dst, load_sem.at[i])
         for i, (src, dst) in enumerate(
@@ -160,15 +168,8 @@
             )
         )
     ]
-    for load in loads:
+    for load in loads[:2]:
         load.start()
-
-    barrier = pltpu.get_barrier_semaphore()
-    peers = [pair, xpart]
-    peers += [at_z((z + o) % NZ) for o in range(1, NZ)]
-    peers += [at_mp((mp + o) % 8) for o in range(1, 8)]
-    for device in peers:
-        pl.semaphore_signal(barrier, inc=1, device_id=device, device_id_type=MESH)
 
     def slot_of(block):
         plane, off = block
@@ -188,9 +189,9 @@
 
     def piece(p, slot):
         if p == 0:
-            return gath6.at[slot, pl.ds(0, 64)]
+            return gath6.at[slot, pl.ds(0, 80)]
         if p == 1:
-            return gath6.at[slot, pl.ds(64, 48)]
+            return gath6.at[slot, pl.ds(80, 32)]
         return gathg.at[slot]
 
     wtargets = (zup, zdown, xpart)
@@ -217,6 +218,8 @@
             send_w(0, k, p)
     for p in range(3):
         send_pair(OWN, (0, 0), p)
+    for load in loads[2:]:
+        load.start()
 
     def column(row):
         a = lax.broadcasted_iota(jnp.int32, (112, 112), 0)
@@ -237,23 +240,30 @@
 
     ysends = []
     relays = []
-    relayed = 0
-
-    def compute(unit, block):
+
+    SUBS = ((0, 80), (80, 64))
+
+    def compute(unit, block, sub):
         slot = slot_of(block)
-        for p in range(3):
+        lo, n = SUBS[sub]
+        for p in ((0,), (1, 2))[sub]:
             ref = piece(p, slot + 1 - c)
             rcopy(ref, ref, psend_sem.at[p, unit], precv_sem.at[p, unit], pair).wait_recv()
-        six = nt(gath6[pl.ds(slot, 2)].reshape(224, 1664), rows6[...])
-        giant = nt(gathg[pl.ds(slot, 2)].reshape(96, 768), rowsg[...])
-        for cc in range(2):
-            a = six[112 * cc : 112 * cc + 112]
-            b = giant[48 * cc : 48 * cc + 48]
-            part[slot + cc, 0:96, :] = a[0:96].astype(BF16)
-            part[slot + cc, 96:112, :] = (a[96:112] + b[0:16]).astype(BF16)
-            part[slot + cc, 112:144, :] = b[16:48].astype(BF16)
+        if sub == 0:
+            six = nt(gath6[pl.ds(slot, 2), 0:80].reshape(160, 1664), rows6[...])
+            part[pl.ds(slot, 2), 0:80, :] = six.astype(BF16).reshape(2, 80, 336)
+        else:
+            six = nt(gath6[pl.ds(slot, 2), 80:112].reshape(64, 1664), rows6[...])
+            giant = nt(gathg[pl.ds(slot, 2)].reshape(96, 768), rowsg[...])
+            for cc in range(2):
+                a = six[32 * cc : 32 * cc + 32]
+                b = giant[48 * cc : 48 * cc + 48]
+                part[slot + cc, 80:96, :] = a[0:16].astype(BF16)
+                part[slot + cc, 96:112, :] = (a[16:32] + b[0:16]).astype(BF16)
+                part[slot + cc, 112:144, :] = b[16:48].astype(BF16)
         role = (y - slot // 8 + NY) % NY
         u = (slot // 2) % 4
+        rows = pl.ds(lo, n)
 
         def send(cond, src, dst, ssem, rsem, device):
             @pl.when(cond)
@@ -262,25 +272,29 @@
 
             ysends.append((cond, lambda: rcopy(src, dst, ssem, rsem, device)))
 
-        first, second = part.at[slot], part.at[slot + 1]
-        send(role == 2, first, yrel.at[unit], ysend_sem.at[unit, 0], yrel_sem.at[unit], ydown)
-        send(role == 2, second, yrel.at[unit], ysend_sem.at[unit, 1], yrel_sem.at[unit], yup)
-        send(role == 1, second, yrecv.at[0, u, 1], ysend_sem.at[unit, 0], yrecv_sem.at[0, u, 1], ydown)
-        send(role == 3, first, yrecv.at[1, u, 0], ysend_sem.at[unit, 0], yrecv_sem.at[1, u, 0], yup)
+        first, second = part.at[slot, rows], part.at[slot + 1, rows]
+        rel, rsem = yrel.at[unit, rows], yrel_sem.at[sub, unit]
+        s0, s1 = ysend_sem.at[sub, unit, 0], ysend_sem.at[sub, unit, 1]
+        send(role == 2, first, rel, s0, rsem, ydown)
+        send(role == 2, second, rel, s1, rsem, yup)
+        send(role == 1, second, yrecv.at[0, u, 1, rows], s0, yrecv_sem.at[sub, 0, u, 1], ydown)
+        send(role == 3, first, yrecv.at[1, u, 0, rows], s0, yrecv_sem.at[sub, 1, u, 0], yup)
 
         def relay():
             for want, cc, side, device in ((1, 0, 0, ydown), (3, 1, 1, yup)):
-                src, dst = part.at[slot + cc], yrecv.at[side, u, cc]
-                ssem, rsem = ysend_sem.at[unit, 1], yrecv_sem.at[side, u, cc]
+
+                def descriptor(cc=cc, side=side, device=device):
+                    dst = yrecv.at[side, u, cc, rows]
+                    return rcopy(part.at[slot + cc, rows], dst, s1, yrecv_sem.at[sub, side, u, cc], device)
 
                 @pl.when(role == want)
-                def _(cc=cc, src=src, dst=dst, ssem=ssem, rsem=rsem, device=device):
-                    ref = yrel.at[unit]
-                    rcopy(ref, ref, ssem, yrel_sem.at[unit], device).wait_recv()
-                    part[slot + cc] = (part[slot + cc].astype(F32) + yrel[unit].astype(F32)).astype(BF16)
-                    rcopy(src, dst, ssem, rsem, device).start()
-
-                ysends.append((role == want, lambda src=src, dst=dst, ssem=ssem, rsem=rsem, device=device: rcopy(src, dst, ssem, rsem, device)))
+                def _(cc=cc, device=device, descriptor=descriptor):
+                    rcopy(rel, rel, s1, rsem, device).wait_recv()
+                    both = part[slot + cc, lo : lo + n].astype(F32) + yrel[unit, lo : lo + n].astype(F32)
+                    part[slot + cc, lo : lo + n] = both.astype(BF16)
+                    descriptor().start()
+
+                ysends.append((role == want, descriptor))
 
         relays.append(relay)
 
@@ -313,75 +327,94 @@
     work += [functools.partial(residuals, i) for i in range(3)]
     work += [functools.partial(turn_heads, 0, 6), functools.partial(turn_heads, 6, 11)]
 
+    def run_relays(keep_back):
+        while len(relays) > keep_back:
+            relays.pop(0)()
+
     for s in range(STEPS):
-        for p in range(3):
-            for k in range(3):
-                wait_w(s, k, p)
-            if s + 1 < STEPS:
+        for ps in ((0,), (1, 2)):
+            for p in ps:
                 for k in range(3):
-                    send_w(s + 1, k, p)
-            for k in range(3):
-                send_pair(3 * s + k, RECVS[s][k], p)
-            if s > 0:
-                compute(3 * (s - 1) + p, RECVS[s - 1][p])
-            elif p == 0:
-                pick_rows(2)
-            elif p == 1:
-                compute(OWN, (0, 0))
-            if p != (1 if s == 0 else 2) and s + p > 0 and work:
+                    wait_w(s, k, p)
+                if s + 1 < STEPS:
+                    for k in range(3):
+                        send_w(s + 1, k, p)
+                for k in range(3):
+                    send_pair(3 * s + k, RECVS[s][k], p)
+            if ps == (0,):
+                if s == 0:
+                    pick_rows(2)
+                    compute(OWN, (0, 0), 0)
+                    compute(OWN, (0, 0), 1)
+                else:
+                    for k in range(3):
+                        compute(3 * (s - 1) + k, RECVS[s - 1][k], 1)
+                run_relays(3)
+                for k in range(3):
+                    compute(3 * s + k, RECVS[s][k], 0)
+            elif s + 1 < STEPS:
                 work.pop(0)()
-            while len(relays) - relayed > 2:
-                relays[relayed]()
-                relayed += 1
-    while work:
-        work.pop(0)()
-
-    def summed(u, cc):
-        total = part[y * 8 + u * 2 + cc].astype(F32)
+                work.pop(0)()
+                run_relays(3)
+
+    def summed(u, cc, sub):
+        lo, n = SUBS[sub]
+        total = part[y * 8 + u * 2 + cc, lo : lo + n].astype(F32)
         for side in range(2):
-            total = total + yrecv[side, u, cc].astype(F32)
+            total = total + yrecv[side, u, cc, lo : lo + n].astype(F32)
         return total
 
-    def wait_y(u):
+    def wait_y(u, sub):
         for side in range(2):
             for cc in range(2):
-                ref = yrecv.at[side, u, cc]
-                rcopy(ref, ref, ysend_sem.at[0, 0], yrecv_sem.at[side, u, cc], xhpart).wait_recv()
-
-    def xh_copy(k):
-        return rcopy(xsend.at[k], xrecv.at[k], xh_sem.at[0, k], xh_sem.at[1, k], xhpart)
-
-    def exchange():
+                ref = yrecv.at[side, u, cc, pl.ds(*SUBS[sub])]
+                rcopy(ref, ref, ysend_sem.at[0, 0, 0], yrecv_sem.at[sub, side, u, cc], xhpart).wait_recv()
+
+    def xh_copy(k, sub):
+        rows = pl.ds(*SUBS[sub])
+        src, dst = xsend.at[k, pl.ds(0, 2), rows], xrecv.at[k, pl.ds(0, 2), rows]
+        return rcopy(src, dst, xh_sem.at[0, k, sub], xh_sem.at[1, k, sub], xhpart)
+
+    def exchange(sub):
+        lo, n = SUBS[sub]
         for k in range(2):
             u = 2 * (1 - xh) + k
-            wait_y(u)
+            wait_y(u, sub)
             for cc in range(2):
-                xsend[k, cc] = summed(u, cc).astype(BF16)
-            xh_copy(k).start()
-
-    def targets():
+                xsend[k, cc, lo : lo + n] = summed(u, cc, sub).astype(BF16)
+            xh_copy(k, sub).start()
+
+    def targets(sub):
         for k in range(2):
             u = 2 * xh + k
-            wait_y(u)
-            xh_copy(k).wait_recv()
+            wait_y(u, sub)
+            xh_copy(k, sub).wait_recv()
+            lo, n = SUBS[sub]
             for cc in range(2):
-                total = summed(u, cc) + xrecv[k, cc].astype(F32)
+                total = summed(u, cc, sub) + xrecv[k, cc, lo : lo + n].astype(F32)
                 f = 100 * (2 * k + cc)
-                tgt[f : f + 100, :] += total[0:100]
-                f = 400 + 44 * (2 * k + cc)
-                tgt[f : f + 44, :] += total[100:144]
+                if sub == 0:
+                    tgt[f : f + 80, :] += total
+                else:
+                    tgt[f + 80 : f + 100, :] += total[0:20]
+                    f = 400 + 44 * (2 * k + cc)
+                    tgt[f : f + 44, :] += total[20:64]
 
     early = y // 2 == xl
-    for i in range(relayed, len(relays)):
-        relays[i]()
-    relayed = len(relays)
-    pl.when(early)(exchange)
+
+    @pl.when(early)
+    def _():
+        exchange(0)
+        exchange(1)
+
     for k in range(3):
-        compute(3 * (STEPS - 1) + k, RECVS[STEPS - 1][k])
-    for i in range(relayed, len(relays)):
-        relays[i]()
-    pl.when(jnp.logical_not(early))(exchange)
-    targets()
+        compute(3 * (STEPS - 1) + k, RECVS[STEPS - 1][k], 1)
+    run_relays(3)
+    pl.when(jnp.logical_not(early))(functools.partial(exchange, 0))
+    run_relays(0)
+    pl.when(jnp.logical_not(early))(functools.partial(exchange, 1))
+    targets(0)
+    targets(1)
 
     def sums(lo, hi):
         t = tgt[lo:hi, :]
@@ -421,7 +454,6 @@
 
     cos6 = gradient(0, 400, 0)
     cosg = gradient(400, 576, 3)
-    grad[576:640, :] = jnp.zeros((64, 336), BF16)
     loss_local = jnp.sum(2.0 - cos6 - cosg, axis=1, keepdims=True)
     lossz[z] = jnp.broadcast_to(loss_local, (8, 128))
     for o in range(1, NZ):
@@ -431,16 +463,25 @@
         pending.append(cp)
 
     order = [(z + o) % NZ for o in Z_ORDER] + [z]
+
+    def head_rows(core):
+        rows = grad[pl.ds(pl.multiple_of(core * 288, 16), 288), :]
+        g = nn(rows, stu[...]).astype(BF16)
+        for x in range(2):
+            for r in range(9):
+                for l in range(11):
+                    t = r * 11 + l
+                    lo = 144 * x + 16 * r
+                    gs[t // 13, 2 * core + x, t % 13] = g[lo : lo + 16, 128 * l : 128 * l + 128]
+            for j in range(8, 13):
+                gs[7, 2 * core + x, j] = jnp.zeros((16, 128), BF16)
+
+    head_rows(1 - c)
     for kk in order:
-        rows = grad[pl.ds(pl.multiple_of(kk * 80, 16), 80), :]
-        g = nn(rows, stu[...]).astype(BF16)
-        for q in range(3):
-            gs[kk, q] = g[:, 384 * q : 384 * q + 384]
-        gs[kk, 3, :, 0:256] = g[:, 1152:1408]
-        gs[kk, 3, :, 256:384] = jnp.zeros((80, 128), BF16)
         cp = rcopy(gs.at[kk, pl.ds(2 * (1 - c), 2)], grecv.at[kk], g_sem.at[0, kk], g_sem.at[1, kk], pair)
         cp.start()
         pending.append(cp)
+    head_rows(c)
 
     for kk in order:
         rcopy(grecv.at[kk], grecv.at[kk], g_sem.at[0, kk], g_sem.at[1, kk], pair).wait_recv()
@@ -451,9 +492,8 @@
 
     def back_pair(t):
         yy = (y + t) % NY
-        for j in range(2):
-            rows = pmat[pl.ds(pl.multiple_of((yy * 2 + j) * 176, 16), 176), :]
-            bsend[yy, j] = nn(rows, grad[0:576, :]).astype(BF16)
+        rows = pmat[pl.ds(pl.multiple_of(yy * 352, 16), 352), :]
+        bsend[yy] = nn(rows, grad[...]).astype(BF16).reshape(2, 176, 336)
         if t:
             o = (3 - t) % NY
             cp = rcopy(bsend.at[yy], byr.at[o], b_sem.at[0, t], b_sem.at[1, o], at_mp(yy * 2 + xh))
@@ -512,11 +552,15 @@
         cp.start()
         pending.append(cp)
 
+    def ag_z(ref, sid, rsem, off):
+        ag_send(ref, agz_sem.at[0, sid], rsem, at_z((z + off + NZ) % NZ))
+
     mine = ag.at[z, q_own]
-    for o in Z_ORDER:
-        zz = (z + o) % NZ
-        ag_send(mine, agz_sem.at[0, zz], agz_sem.at[1, z], at_z(zz))
+    ag_z(mine, 0, agz_sem.at[1, z], 1)
+    ag_z(mine, 1, agz_sem.at[1, z], -1)
     ag_send(mine, agx_sem.at[0, z], agx_sem.at[1, z], xpart)
+    ag_z(mine, 2, agz_sem.at[1, z], 2)
+    ag_z(mine, 3, agz_sem.at[1, z], -2)
     ag_send(mine, agp_sem.at[0, z, xl], agp_sem.at[1, z, xl], pair)
 
     rcopy(lossx.at[0], lossx.at[1], l_sem.at[2, 0], l_sem.at[2, 1], xpart).wait_recv()
@@ -528,38 +572,62 @@
     v = back_sum(xh) + bxr[...].astype(F32)
     for i in range(3):
         bfin[i] = v[:, 112 * i : 112 * i + 112]
-    back_store = pltpu.make_async_copy(bfin, back_out, out_sem.at[8, 0])
+    back_store = pltpu.make_async_copy(bfin, back_out, out_sem.at[2])
     back_store.start()
 
-    zs = [z] + [(z + o) % NZ for o in (1, 7, 2, 6, 3, 5, 4)]
-    for zz in zs:
-        if zz is not z:
-            ref = ag.at[zz, q_own]
-            rcopy(ref, ref, agz_sem.at[0, zz], agz_sem.at[1, zz], at_z(zz)).wait_recv()
+    def from_z(off):
+        zz = (z + off + NZ) % NZ
+        ref = ag.at[zz, q_own]
+        rcopy(ref, ref, agz_sem.at[0, 0], agz_sem.at[1, zz], pair).wait_recv()
+        if off == -2:
+            ag_z(ref, 4, agz_sem.at[1, zz], 2)
+            ag_z(ref, 5, agz_sem.at[1, zz], 1)
+        if off == 2:
+            ag_z(ref, 6, agz_sem.at[1, zz], -1)
+        if off != 1:
             ag_send(ref, agx_sem.at[0, zz], agx_sem.at[1, zz], xpart)
-            ag_send(ref, agp_sem.at[0, zz, xl], agp_sem.at[1, zz, xl], pair)
-    for zz in zs:
+        ag_send(ref, agp_sem.at[0, zz, xl], agp_sem.at[1, zz, xl], pair)
+
+    def from_x(off):
+        zz = (z + off + NZ) % NZ
         ref = ag.at[zz, q_x]
         rcopy(ref, ref, agx_sem.at[0, zz], agx_sem.at[1, zz], xpart).wait_recv()
+        if off == 0:
+            ag_z(ref, 7, agx_sem.at[1, zz], -1)
         ag_send(ref, agp_sem.at[0, zz, 1 - xl], agp_sem.at[1, zz, 1 - xl], pair)
+
+    from_z(-1)
+    from_z(1)
+    from_x(0)
+    from_z(-2)
+    from_z(2)
+    from_x(-1)
+    from_z(-3)
+    from_z(3)
+    from_x(1)
+    from_z(-4)
+    for off in (-2, 2, -3, 3, -4):
+        from_x(off)
 
     rcopy(lossc.at[0], lossc.at[1], l_sem.at[3, 0], l_sem.at[3, 1], pair).wait_recv()
     loss_out[...] = (lossc[0, 0:1, 0:1] + lossc[1, 0:1, 0:1]) / token_total
 
-    stores = [back_store]
     for zz in range(NZ):
         for x in range(2):
             ref = ag.at[zz, 2 * (1 - c) + x]
             rcopy(ref, ref, agp_sem.at[0, zz, x], agp_sem.at[1, zz, x], pair).wait_recv()
-        n = 80 if zz < 7 else 16
-        out, lo = (gp6_out, 80 * zz) if zz < 5 else (gpg_out, 80 * zz - 400)
         for q in range(4):
-            w = 384 if q < 3 else 256
-            cp = pltpu.make_async_copy(
-                ag.at[zz, q, pl.ds(0, n), pl.ds(0, w)], out.at[pl.ds(lo, n), pl.ds(384 * q, w)], out_sem.at[zz, q]
-            )
-            cp.start()
-            stores.append(cp)
+            for j in range(13 if zz < 7 else 8):
+                r, l = divmod(zz * 13 + j, 11)
+                lo = 144 * q + 16 * r
+                fout[lo : lo + 16, 128 * l : 128 * l + 128] = ag[zz, q, j]
+    stores = [
+        back_store,
+        pltpu.make_async_copy(fout.at[pl.ds(0, 400)], gp6_out, out_sem.at[0]),
+        pltpu.make_async_copy(fout.at[pl.ds(400, 176)], gpg_out, out_sem.at[1]),
+    ]
+    stores[1].start()
+    stores[2].start()
 
     for away, descriptor in ysends:
 
@@ -568,7 +636,8 @@
             descriptor().wait_send()
 
     for k in range(2):
-        xh_copy(k).wait_send()
+        for sub in range(2):
+            xh_copy(k, sub).wait_send()
     for cp in pending:
         cp.wait_send()
     for cp in stores:
@@ -614,14 +683,15 @@
         pltpu.VMEM((576, 336), F32),
         pltpu.VMEM((576, 336), F32),
         pltpu.VMEM((8, 8, 336), F32),
-        pltpu.VMEM((640, 336), BF16),
-        pltpu.VMEM((NZ, 4, 80, 384), BF16),
-        pltpu.VMEM((NZ, 2, 80, 384), BF16),
-        pltpu.VMEM((NZ, 80, 384), BF16),
-        pltpu.VMEM((NZ, 80, 384), BF16),
-        pltpu.VMEM((NZ, 80, 384), BF16),
-        pltpu.VMEM((NZ, 80, 384), BF16),
-        pltpu.VMEM((NZ, 4, 80, 384), BF16),
+        pltpu.VMEM((576, 336), BF16),
+        pltpu.VMEM((NZ, 4, 13, 16, 128), BF16),
+        pltpu.VMEM((NZ, 2, 13, 16, 128), BF16),
+        pltpu.VMEM((NZ, 13, 16, 128), BF16),
+        pltpu.VMEM((NZ, 13, 16, 128), BF16),
+        pltpu.VMEM((NZ, 13, 16, 128), BF16),
+        pltpu.VMEM((NZ, 13, 16, 128), BF16),
+        pltpu.VMEM((NZ, 4, 13, 16, 128), BF16),
+        pltpu.VMEM((576, 1408), BF16),
         pltpu.VMEM((NY, 2, 176, 336), BF16),
         pltpu.VMEM((3, 2, 176, 336), BF16),
         pltpu.VMEM((176, 336), BF16),
@@ -635,18 +705,18 @@
         dma((3, 15)),
         dma((3, 16)),
         dma((3, 16)),
-        dma((16, 2)),
-        dma((2, 4, 2)),
-        dma((16,)),
-        dma((2, 2)),
+        dma((2, 16, 2)),
+        dma((2, 2, 4, 2)),
+        dma((2, 16)),
+        dma((2, 2, 2)),
         dma((2, 8)),
         dma((6, 8)),
-        dma((2, 8)),
+        dma((3, 8)),
         dma((2, 8)),
         dma((2, 8, 2)),
         dma((3, 4)),
         dma((4, 8)),
-        dma((9, 4)),
+        dma((3,)),
     ]
     gp6, gpg, back, loss = pl.pallas_call(
         functools.partial(kernel, token_total),

time: 152 us -> 139 us (0.914)
  Pallas kernels: 144 us -> 132 us
    pallas_call x1, Pallas kernels: 144 us -> 132 us  [local(): pl.pallas_call(functools.partial(kernel, token_total), out_shape=(jax.Sha...]
where the time goes in v3:
time: 139 us
  Pallas kernels  132 us (95%)
  other arithmetic  3.85 us (3%)
  between operations  2.43 us (2%)
    pallas_call x1, Pallas kernels, local(): pl.pallas_call(functools.partial(kernel, token_total), out_shape=(jax.Sha...  132 us
    transpose x1, other arithmetic, local(): gp6.astype(F32)  2.84 us

profile of v3, /device:TPU:1, one launch (start us, length us, event | category | flops | bytes accessed | tf_op | source)
XLA Modules:
  0.0 138.8 jit_solution(403865505043904196)
XLA Ops:
  0.6 131.8 %shard_map.129 = (bf16[400,1408]{1,0:T(8,128)(2,1)}, bf16[176,1408]{1,0:T(8,128)(2,1)}, f32[3,176,112]{2,1,0:T(8,128)}, f32[1,1]{1,0:T(1,128)}) custom-call(s32[3,112]{1,0:T(4,128)} %keep.1, bf16[336,1408]{1,0:T(8,128)(2,1)} %bitcast.16, bf16[3,560,1600]{2,1,0:T(8,128)(2,1)} %h6_hbm.1, bf16[3,400,560]{2,1,0:T(8,128)(2,1)} %bitcast.14, ...), custom_call_target="tpu_custom_call" | custom-call | flops 6000000000 | bytes 20000000 | tf_op jit(solution)/shard_map/pallas_call | solution.py:721
  132.4 0.0 copy-start
  132.5 0.0 copy-start.1
  132.5 2.8 %convert_bitcast_fusion = f32[1408,400]{0,1:T(8,128)} fusion(bf16[400,1408]{1,0:T(8,128)(2,1)} %get-tuple-element.9), kind=kLoop, calls=%fused_computation | loop fusion | flops 563200 | bytes 3379200 | tf_op jit(solution)/shard_map/transpose | solution.py:748
  135.3 0.0 copy-done
  135.3 1.0 convert_bitcast_fusion.1
  136.3 0.0 copy-done.1
  136.3 0.7 copy.16
Async XLA Ops:
  132.4 2.9 %copy-start = (bf16[176,1408]{1,0:T(8,128)(2,1)S(1)}, bf16[176,1408]{1,0:T(8,128)(2,1)}, u32[]{:S(2)}) copy-start(bf16[176,1408]{1,0:T(8,128)(2,1)} %get-tuple-element.10) | copy-start | bytes 1486852
  132.5 3.9 %copy-start.1 = (f32[3,176,112]{2,1,0:T(8,128)S(1)}, f32[3,176,112]{2,1,0:T(8,128)}, u32[]{:S(2)}) copy-start(f32[3,176,112]{2,1,0:T(8,128)} %get-tuple-element.8) | copy-start | bytes 709636

commit v4 on v3

--- a/solution.py
+++ b/solution.py
@@ -33,7 +33,6 @@
 )
 STEPS = len(SENDS)
 OWN = 3 * STEPS
-Z_ORDER = (4, 3, 5, 2, 6, 1, 7)
 
 
 def nt(a, b):
@@ -46,7 +45,7 @@
 
 def kernel(
     token_total,
-    keep,
+    keep_hbm,
     stu_hbm,
     h6_hbm,
     r6_hbm,
@@ -60,6 +59,7 @@
     gpg_out,
     back_out,
     loss_out,
+    keep,
     w6_in,
     wg_in,
     gath6,
@@ -99,6 +99,7 @@
     lossz,
     lossx,
     lossc,
+    lossv,
     load_sem,
     wsend_sem,
     wrecv_sem,
@@ -165,6 +166,7 @@
                 (pg_hbm, pt.at[pl.ds(400, 176)]),
                 (r6_hbm, r6),
                 (rg_hbm, rg),
+                (keep_hbm, keep),
             )
         )
     ]
@@ -175,17 +177,6 @@
         plane, off = block
         pl_ = xl if plane == 0 else 1 - xl
         return pl_ * 2 * NZ + ((z + off + NZ) % NZ) * 2
-
-    own = dp
-    loads[0].wait()
-    loads[1].wait()
-    gath6[own] = jnp.zeros((112, 1664), BF16)
-    gath6[own, 0:100, 0:1600] = w6_in[...]
-    wpad[0:4, :] = jnp.zeros((4, 768), F32)
-    wpad[4:48, :] = wg_in[...].astype(F32)
-    gathg[own] = wpad[...].astype(BF16)
-
-    pl.semaphore_wait(barrier, len(peers))
 
     def piece(p, slot):
         if p == 0:
@@ -213,9 +204,21 @@
         ref = piece(p, slot_of(RECVS[s][k]) + c)
         rcopy(ref, ref, wsend_sem.at[p, 3 * s + k], wrecv_sem.at[p, 3 * s + k], wtargets[k]).wait_recv()
 
-    for p in range(3):
+    own = dp
+    loads[0].wait()
+    gath6[own, 96:112, :] = jnp.zeros((16, 1664), BF16)
+    gath6[own, 0:96, 1536:1664] = jnp.zeros((96, 128), BF16)
+    gath6[own, 0:100, 0:1600] = w6_in[...]
+    pl.semaphore_wait(barrier, len(peers))
+    for p in range(2):
         for k in range(3):
             send_w(0, k, p)
+    loads[1].wait()
+    wpad[0:4, :] = jnp.zeros((4, 768), F32)
+    wpad[4:48, :] = wg_in[...].astype(F32)
+    gathg[own] = wpad[...].astype(BF16)
+    for k in range(3):
+        send_w(0, k, 2)
     for p in range(3):
         send_pair(OWN, (0, 0), p)
     for load in loads[2:]:
@@ -235,6 +238,7 @@
 
     loads[2].wait()
     loads[3].wait()
+    loads[9].wait()
     pick_rows(0)
     pick_rows(1)
 
@@ -243,24 +247,36 @@
 
     SUBS = ((0, 80), (80, 64))
 
-    def compute(unit, block, sub):
-        slot = slot_of(block)
+    def compute(items, sub):
+        slots = [slot_of(block) for unit, block in items]
+        for (unit, block), slot in zip(items, slots):
+            for p in ((0,), (1, 2))[sub]:
+                ref = piece(p, slot + 1 - c)
+                rcopy(ref, ref, psend_sem.at[p, unit], precv_sem.at[p, unit], pair).wait_recv()
+
+        def rows_of(ref, lo, hi):
+            blocks = [ref[pl.ds(slot, 2), lo:hi].reshape(2 * (hi - lo), ref.shape[2]) for slot in slots]
+            return jnp.concatenate(blocks, axis=0)
+
+        if sub == 0:
+            six = nt(rows_of(gath6, 0, 80), rows6[...]).astype(BF16)
+            for i, slot in enumerate(slots):
+                part[pl.ds(slot, 2), 0:80, :] = six[160 * i : 160 * i + 160].reshape(2, 80, 336)
+        else:
+            six = nt(rows_of(gath6, 80, 112), rows6[...])
+            giant = nt(rows_of(gathg, 0, 48), rowsg[...])
+            for i, slot in enumerate(slots):
+                for cc in range(2):
+                    a = six[64 * i + 32 * cc : 64 * i + 32 * cc + 32]
+                    b = giant[96 * i + 48 * cc : 96 * i + 48 * cc + 48]
+                    part[slot + cc, 80:96, :] = a[0:16].astype(BF16)
+                    part[slot + cc, 96:112, :] = (a[16:32] + b[0:16]).astype(BF16)
+                    part[slot + cc, 112:144, :] = b[16:48].astype(BF16)
+        for (unit, block), slot in zip(items, slots):
+            pass_round(unit, slot, sub)
+
+    def pass_round(unit, slot, sub):
         lo, n = SUBS[sub]
-        for p in ((0,), (1, 2))[sub]:
-            ref = piece(p, slot + 1 - c)
-            rcopy(ref, ref, psend_sem.at[p, unit], precv_sem.at[p, unit], pair).wait_recv()
-        if sub == 0:
-            six = nt(gath6[pl.ds(slot, 2), 0:80].reshape(160, 1664), rows6[...])
-            part[pl.ds(slot, 2), 0:80, :] = six.astype(BF16).reshape(2, 80, 336)
-        else:
-            six = nt(gath6[pl.ds(slot, 2), 80:112].reshape(64, 1664), rows6[...])
-            giant = nt(gathg[pl.ds(slot, 2)].reshape(96, 768), rowsg[...])
-            for cc in range(2):
-                a = six[32 * cc : 32 * cc + 32]
-                b = giant[48 * cc : 48 * cc + 48]
-                part[slot + cc, 80:96, :] = a[0:16].astype(BF16)
-                part[slot + cc, 96:112, :] = (a[16:32] + b[0:16]).astype(BF16)
-                part[slot + cc, 112:144, :] = b[16:48].astype(BF16)
         role = (y - slot // 8 + NY) % NY
         u = (slot // 2) % 4
         rows = pl.ds(lo, n)
@@ -300,7 +316,7 @@
 
     def head_out(i):
         if i == 0:
-            for load in loads[4:]:
+            for load in loads[4:9]:
                 load.wait()
         outs[192 * i : 192 * i + 192, :] = nt(pt[192 * i : 192 * i + 192, :], stu[...])
 
@@ -327,6 +343,9 @@
     work += [functools.partial(residuals, i) for i in range(3)]
     work += [functools.partial(turn_heads, 0, 6), functools.partial(turn_heads, 6, 11)]
 
+    def step_units(s):
+        return [(3 * s + k, RECVS[s][k]) for k in range(3)]
+
     def run_relays(keep_back):
         while len(relays) > keep_back:
             relays.pop(0)()
@@ -344,14 +363,12 @@
             if ps == (0,):
                 if s == 0:
                     pick_rows(2)
-                    compute(OWN, (0, 0), 0)
-                    compute(OWN, (0, 0), 1)
+                    compute([(OWN, (0, 0))], 0)
+                    compute([(OWN, (0, 0))], 1)
                 else:
-                    for k in range(3):
-                        compute(3 * (s - 1) + k, RECVS[s - 1][k], 1)
+                    compute(step_units(s - 1), 1)
                 run_relays(3)
-                for k in range(3):
-                    compute(3 * s + k, RECVS[s][k], 0)
+                compute(step_units(s), 0)
             elif s + 1 < STEPS:
                 work.pop(0)()
                 work.pop(0)()
@@ -402,15 +419,10 @@
 
     early = y // 2 == xl
 
-    @pl.when(early)
-    def _():
-        exchange(0)
-        exchange(1)
-
-    for k in range(3):
-        compute(3 * (STEPS - 1) + k, RECVS[STEPS - 1][k], 1)
-    run_relays(3)
-    pl.when(jnp.logical_not(early))(functools.partial(exchange, 0))
+    run_relays(0)
+    compute(step_units(STEPS - 1), 1)
+    exchange(0)
+    pl.when(early)(functools.partial(exchange, 1))
     run_relays(0)
     pl.when(jnp.logical_not(early))(functools.partial(exchange, 1))
     targets(0)
@@ -462,7 +474,8 @@
         cp.start()
         pending.append(cp)
 
-    order = [(z + o) % NZ for o in Z_ORDER] + [z]
+    offsets = (-4, -3, 3, 1, -2, 2, -1, 0)
+    at = {off: (z + off + NZ) % NZ for off in offsets}
 
     def head_rows(core):
         rows = grad[pl.ds(pl.multiple_of(core * 288, 16), 288), :]
@@ -477,18 +490,37 @@
                 gs[7, 2 * core + x, j] = jnp.zeros((16, 128), BF16)
 
     head_rows(1 - c)
-    for kk in order:
+    for kk in at.values():
         cp = rcopy(gs.at[kk, pl.ds(2 * (1 - c), 2)], grecv.at[kk], g_sem.at[0, kk], g_sem.at[1, kk], pair)
         cp.start()
         pending.append(cp)
     head_rows(c)
 
-    for kk in order:
-        rcopy(grecv.at[kk], grecv.at[kk], g_sem.at[0, kk], g_sem.at[1, kk], pair).wait_recv()
-        gxs[kk] = (gs[kk, 2 * c + 1 - xl].astype(F32) + grecv[kk, 1 - xl].astype(F32)).astype(BF16)
+    def both_cores(kk, x):
+        return gs[kk, 2 * c + x].astype(F32) + grecv[kk, x].astype(F32)
+
+    def to_x(kk):
         cp = rcopy(gxs.at[kk], gxr.at[kk], g_sem.at[2, kk], g_sem.at[3, kk], xpart)
         cp.start()
         pending.append(cp)
+
+    def z_hop(src, sid, step):
+        cp = rcopy(src, gzr.at[sid], g_sem.at[4, sid], g_sem.at[5, sid], at_z((z + step + NZ) % NZ))
+        cp.start()
+        pending.append(cp)
+
+    def from_hop(sid):
+        rcopy(gzr.at[sid], gzr.at[sid], g_sem.at[4, sid], g_sem.at[5, sid], pair).wait_recv()
+        return gzr[sid].astype(F32)
+
+    for off, kk in at.items():
+        rcopy(grecv.at[kk], grecv.at[kk], g_sem.at[0, kk], g_sem.at[1, kk], pair).wait_recv()
+        if off:
+            gxs[kk] = both_cores(kk, 1 - xl).astype(BF16)
+            if off == 1:
+                z_hop(gxs.at[kk], 7, 1)
+            else:
+                to_x(kk)
 
     def back_pair(t):
         yy = (y + t) % NY
@@ -500,18 +532,31 @@
             cp.start()
             pending.append(cp)
 
-    for t in (2, 1, 3, 0):
-        back_pair(t)
-
-    gz_pending = []
-    for kk in order:
-        rcopy(gxr.at[kk], gxr.at[kk], g_sem.at[2, kk], g_sem.at[3, kk], xpart).wait_recv()
-        v = gs[kk, 2 * c + xl].astype(F32) + grecv[kk, xl].astype(F32) + gxr[kk].astype(F32)
-        gzs[kk] = v.astype(BF16)
-        if kk is not z:
-            cp = rcopy(gzs.at[kk], gzr.at[z], g_sem.at[4, kk], g_sem.at[5, z], at_z(kk))
-            cp.start()
-            pending.append(cp)
+    def own_part(off):
+        kk = at[off]
+        v = both_cores(kk, xl)
+        if off != 1:
+            rcopy(gxr.at[kk], gxr.at[kk], g_sem.at[2, kk], g_sem.at[3, kk], xpart).wait_recv()
+            v = v + gxr[kk].astype(F32)
+        return v
+
+    def pass_on(off, value, sid, step):
+        gzs[at[off]] = value.astype(BF16)
+        z_hop(gzs.at[at[off]], sid, step)
+
+    pass_on(1, own_part(1), 4, 1)
+    back_pair(2)
+    back_pair(1)
+    gxs[z] = (both_cores(z, 1 - xl) + from_hop(7)).astype(BF16)
+    to_x(z)
+    pass_on(-4, own_part(-4), 0, -2)
+    pass_on(-3, own_part(-3), 1, -1)
+    pass_on(3, own_part(3), 2, 1)
+    back_pair(3)
+    back_pair(0)
+    pass_on(-2, own_part(-2) + from_hop(0) + from_hop(1), 5, -2)
+    pass_on(2, own_part(2) + from_hop(2), 6, 2)
+    pass_on(-1, own_part(-1), 3, -1)
 
     for o in range(1, NZ):
         zz = (z + o) % NZ
@@ -538,11 +583,9 @@
     bcp.start()
     pending.append(bcp)
 
-    total = gzs[z].astype(F32)
-    for o in range(1, NZ):
-        zz = (z + o) % NZ
-        rcopy(gzr.at[zz], gzr.at[zz], g_sem.at[4, zz], g_sem.at[5, zz], at_z(zz)).wait_recv()
-        total = total + gzr[zz].astype(F32)
+    total = own_part(0)
+    for sid in (4, 3, 6, 5):
+        total = total + from_hop(sid)
     q_own = 2 * c + xl
     q_x = 2 * c + 1 - xl
     ag[z, q_own] = (total * (head_scale / token_total)).astype(BF16)
@@ -562,18 +605,6 @@
     ag_z(mine, 2, agz_sem.at[1, z], 2)
     ag_z(mine, 3, agz_sem.at[1, z], -2)
     ag_send(mine, agp_sem.at[0, z, xl], agp_sem.at[1, z, xl], pair)
-
-    rcopy(lossx.at[0], lossx.at[1], l_sem.at[2, 0], l_sem.at[2, 1], xpart).wait_recv()
-    lossc[0] = lossx[0] + lossx[1]
-    cp = rcopy(lossc.at[0], lossc.at[1], l_sem.at[3, 0], l_sem.at[3, 1], pair)
-    cp.start()
-    pending.append(cp)
-    bcp.wait_recv()
-    v = back_sum(xh) + bxr[...].astype(F32)
-    for i in range(3):
-        bfin[i] = v[:, 112 * i : 112 * i + 112]
-    back_store = pltpu.make_async_copy(bfin, back_out, out_sem.at[2])
-    back_store.start()
 
     def from_z(off):
         zz = (z + off + NZ) % NZ
@@ -601,16 +632,30 @@
     from_x(0)
     from_z(-2)
     from_z(2)
+
+    rcopy(lossx.at[0], lossx.at[1], l_sem.at[2, 0], l_sem.at[2, 1], xpart).wait_recv()
+    lossc[0] = lossx[0] + lossx[1]
+    cp = rcopy(lossc.at[0], lossc.at[1], l_sem.at[3, 0], l_sem.at[3, 1], pair)
+    cp.start()
+    pending.append(cp)
+    bcp.wait_recv()
+    v = back_sum(xh) + bxr[...].astype(F32)
+    for i in range(3):
+        bfin[i] = v[:, 112 * i : 112 * i + 112]
+    back_store = pltpu.make_async_copy(bfin, back_out, out_sem.at[2])
+    back_store.start()
+
     from_x(-1)
     from_z(-3)
     from_z(3)
+    rcopy(lossc.at[0], lossc.at[1], l_sem.at[3, 0], l_sem.at[3, 1], pair).wait_recv()
+    lossv[...] = (lossc[0, 0:1, 0:1] + lossc[1, 0:1, 0:1]) / token_total
+    loss_store = pltpu.make_async_copy(lossv, loss_out, out_sem.at[3])
+    loss_store.start()
     from_x(1)
     from_z(-4)
     for off in (-2, 2, -3, 3, -4):
         from_x(off)
-
-    rcopy(lossc.at[0], lossc.at[1], l_sem.at[3, 0], l_sem.at[3, 1], pair).wait_recv()
-    loss_out[...] = (lossc[0, 0:1, 0:1] + lossc[1, 0:1, 0:1]) / token_total
 
     for zz in range(NZ):
         for x in range(2):
@@ -623,11 +668,12 @@
                 fout[lo : lo + 16, 128 * l : 128 * l + 128] = ag[zz, q, j]
     stores = [
         back_store,
+        loss_store,
         pltpu.make_async_copy(fout.at[pl.ds(0, 400)], gp6_out, out_sem.at[0]),
         pltpu.make_async_copy(fout.at[pl.ds(400, 176)], gpg_out, out_sem.at[1]),
     ]
-    stores[1].start()
     stores[2].start()
+    stores[3].start()
 
     for away, descriptor in ysends:
 
@@ -659,8 +705,8 @@
     token_total = 336 * 32
     dma = pltpu.SemaphoreType.DMA
     hbm = pl.BlockSpec(memory_space=pl.ANY)
-    vmem = pl.BlockSpec(memory_space=pltpu.VMEM)
     scratch = [
+        pltpu.VMEM((3, 112), jnp.int32),
         pltpu.VMEM((100, 1600), BF16),
         pltpu.VMEM((44, 768), BF16),
         pltpu.VMEM((32, 112, 1664), BF16),
@@ -700,7 +746,8 @@
         pltpu.VMEM((NZ, 8, 128), F32),
         pltpu.VMEM((2, 8, 128), F32),
         pltpu.VMEM((2, 8, 128), F32),
-        dma((9,)),
+        pltpu.VMEM((1, 1), F32),
+        dma((10,)),
         dma((3, 15)),
         dma((3, 15)),
         dma((3, 16)),
@@ -716,7 +763,7 @@
         dma((2, 8, 2)),
         dma((3, 4)),
         dma((4, 8)),
-        dma((3,)),
+        dma((4,)),
     ]
     gp6, gpg, back, loss = pl.pallas_call(
         functools.partial(kernel, token_total),
@@ -726,8 +773,8 @@
             jax.ShapeDtypeStruct((3, 176, 112), F32),
             jax.ShapeDtypeStruct((1, 1), F32),
         ),
-        in_specs=[vmem] + [hbm] * 9,
-        out_specs=(hbm, hbm, hbm, vmem),
+        in_specs=[hbm] * 10,
+        out_specs=(hbm, hbm, hbm, hbm),
         scratch_shapes=scratch,
         compiler_params=pltpu.CompilerParams(
             collective_id=0, has_side_effects=True, vmem_limit_bytes=62 * 1024 * 1024

time: 139 us -> 136 us (0.978)
  Pallas kernels: 132 us -> 129 us
    pallas_call x1, Pallas kernels: 132 us -> 129 us  [local(): pl.pallas_call(functools.partial(kernel, token_total), out_shape=(jax.Sha...]
where the time goes in v4:
time: 136 us
  Pallas kernels  129 us (95%)
  other arithmetic  3.85 us (3%)
  between operations  2.43 us (2%)
    pallas_call x1, Pallas kernels, local(): pl.pallas_call(functools.partial(kernel, token_total), out_shape=(jax.Sha...  129 us
    transpose x1, other arithmetic, local(): gp6.astype(F32)  2.84 us

profile of v4, /device:TPU:1, one launch (start us, length us, event | category | flops | bytes accessed | tf_op | source)
XLA Modules:
  0.0 135.6 jit_solution(3480777825562013561)
XLA Ops:
  0.6 128.6 %shard_map.129 = (bf16[400,1408]{1,0:T(8,128)(2,1)}, bf16[176,1408]{1,0:T(8,128)(2,1)}, f32[3,176,112]{2,1,0:T(8,128)}, f32[1,1]{1,0:T(1,128)}) custom-call(s32[3,112]{1,0:T(4,128)} %keep_hbm.1, bf16[336,1408]{1,0:T(8,128)(2,1)} %bitcast.16, bf16[3,560,1600]{2,1,0:T(8,128)(2,1)} %h6_hbm.1, bf16[3,400,560]{2,1,0:T(8,128)(2,1)} %bitcast.14, ...), custom_call_target="tpu_custom_call" | custom-call | flops 6000000000 | bytes 20000000 | tf_op jit(solution)/shard_map/pallas_call | solution.py:768
  129.3 0.0 copy-start
  129.3 0.0 copy-start.1
  129.3 2.8 %convert_bitcast_fusion = f32[1408,400]{0,1:T(8,128)} fusion(bf16[400,1408]{1,0:T(8,128)(2,1)} %get-tuple-element.9), kind=kLoop, calls=%fused_computation | loop fusion | flops 563200 | bytes 3379200 | tf_op jit(solution)/shard_map/transpose | solution.py:795
  132.1 0.0 copy-done
  132.1 1.0 convert_bitcast_fusion.1
  133.1 0.0 copy-done.1
  133.1 0.7 copy.16
Async XLA Ops:
  129.3 2.9 %copy-start = (bf16[176,1408]{1,0:T(8,128)(2,1)S(1)}, bf16[176,1408]{1,0:T(8,128)(2,1)}, u32[]{:S(2)}) copy-start(bf16[176,1408]{1,0:T(8,128)(2,1)} %get-tuple-element.10) | copy-start | bytes 1486852
  129.3 3.9 %copy-start.1 = (f32[3,176,112]{2,1,0:T(8,128)S(1)}, f32[3,176,112]{2,1,0:T(8,128)}, u32[]{:S(2)}) copy-start(f32[3,176,112]{2,1,0:T(8,128)} %get-tuple-element.8) | copy-start | bytes 709636

commit v5 on v4

--- a/solution.py
+++ b/solution.py
@@ -657,15 +657,20 @@
     for off in (-2, 2, -3, 3, -4):
         from_x(off)
 
+    def lay_out(zz, core):
+        for x in range(2):
+            for j in range(13 if zz < 7 else 8):
+                r, l = divmod(zz * 13 + j, 11)
+                rows = pl.ds(pl.multiple_of(288 * core + (144 * x + 16 * r), 16), 16)
+                fout[rows, 128 * l : 128 * l + 128] = ag[zz, 2 * core + x, j]
+
+    for zz in range(NZ):
+        lay_out(zz, c)
     for zz in range(NZ):
         for x in range(2):
             ref = ag.at[zz, 2 * (1 - c) + x]
             rcopy(ref, ref, agp_sem.at[0, zz, x], agp_sem.at[1, zz, x], pair).wait_recv()
-        for q in range(4):
-            for j in range(13 if zz < 7 else 8):
-                r, l = divmod(zz * 13 + j, 11)
-                lo = 144 * q + 16 * r
-                fout[lo : lo + 16, 128 * l : 128 * l + 128] = ag[zz, q, j]
+        lay_out(zz, 1 - c)
     stores = [
         back_store,
         loss_store,

time: 136 us -> 136 us (level)
  no operation moved by 1% of the time
where the time goes in v5:
time: 136 us
  Pallas kernels  129 us (95%)
  other arithmetic  3.85 us (3%)
  between operations  2.43 us (2%)
    pallas_call x1, Pallas kernels, local(): pl.pallas_call(functools.partial(kernel, token_total), out_shape=(jax.Sha...  129 us
    transpose x1, other arithmetic, local(): gp6.astype(F32)  2.84 us

profile of v5, /device:TPU:1, one launch (start us, length us, event | category | flops | bytes accessed | tf_op | source)
XLA Modules:
  0.0 135.6 jit_solution(9284311939554003067)
XLA Ops:
  0.6 128.6 %shard_map.129 = (bf16[400,1408]{1,0:T(8,128)(2,1)}, bf16[176,1408]{1,0:T(8,128)(2,1)}, f32[3,176,112]{2,1,0:T(8,128)}, f32[1,1]{1,0:T(1,128)}) custom-call(s32[3,112]{1,0:T(4,128)} %keep_hbm.1, bf16[336,1408]{1,0:T(8,128)(2,1)} %bitcast.16, bf16[3,560,1600]{2,1,0:T(8,128)(2,1)} %h6_hbm.1, bf16[3,400,560]{2,1,0:T(8,128)(2,1)} %bitcast.14, ...), custom_call_target="tpu_custom_call" | custom-call | flops 6000000000 | bytes 20000000 | tf_op jit(solution)/shard_map/pallas_call | solution.py:773
  129.2 0.0 copy-start
  129.2 0.0 copy-start.1
  129.2 2.8 %convert_bitcast_fusion = f32[1408,400]{0,1:T(8,128)} fusion(bf16[400,1408]{1,0:T(8,128)(2,1)} %get-tuple-element.9), kind=kLoop, calls=%fused_computation | loop fusion | flops 563200 | bytes 3379200 | tf_op jit(solution)/shard_map/transpose | solution.py:800
  132.1 0.0 copy-done
  132.1 1.0 convert_bitcast_fusion.1
  133.1 0.0 copy-done.1
  133.1 0.7 copy.16
Async XLA Ops:
  129.2 2.9 %copy-start = (bf16[176,1408]{1,0:T(8,128)(2,1)S(1)}, bf16[176,1408]{1,0:T(8,128)(2,1)}, u32[]{:S(2)}) copy-start(bf16[176,1408]{1,0:T(8,128)(2,1)} %get-tuple-element.10) | copy-start | bytes 1486852
  129.2 3.9 %copy-start.1 = (f32[3,176,112]{2,1,0:T(8,128)S(1)}, f32[3,176,112]{2,1,0:T(8,128)}, u32[]{:S(2)}) copy-start(f32[3,176,112]{2,1,0:T(8,128)} %get-tuple-element.8) | copy-start | bytes 709636
